TPU v7x, 256 devices: a whole 4x4x8 slice. The times are simulated.
256 devices in a mesh: row: 32 (over z, x_lo, core), col: 8 (over x_hi, y).
Axes of the slice: x: 4 (x_hi: 2, x_lo: 2; x = x_hi * 2 + x_lo), y: 4, z: 8, core: 2. Of those that a mesh axis runs over, the one named last changes fastest.
Arguments:
- pair_in: bfloat16 [64, 1024, 1024], P(None, 'row', 'col'), may hold values from -6 to 6
- row_feat: bfloat16 [64, 1024], P('col', 'row'), may hold values from -4 to 4
- col_feat: bfloat16 [64, 1024], P('row', 'col'), may hold values from -4 to 4
- cotangent: bfloat16 [64, 1024, 1024], P(None, 'row', 'col'), may hold values from -6 to 6
- conv_weight: bfloat16 [9, 64, 64], replicated, may hold values from -0.25 to 0.25
- norm_gain: float32 [64], replicated, may hold values from 0.25 to 1.75
- norm_shift: float32 [64], replicated, may hold values from -1 to 1
- proj_weight: bfloat16 [64, 64], replicated, may hold values from -0.75 to 0.75
Outputs:
- pair_grad: bfloat16 [64, 1024, 1024], P(None, 'row', 'col')
- row_grad: float32 [64, 1024], P('col', 'row')
- col_grad: float32 [64, 1024], P('row', 'col')
- conv_grad: float32 [9, 64, 64], replicated
- proj_grad: float32 [64, 64], replicated
- gain_grad: float32 [64], replicated
- shift_grad: float32 [64], replicated
All inputs are finite; a program needn't handle non-finite values.
Results may differ from a plain program's by a relative error of at most 0.019.
Values may be sent and summed in bfloat16 or wider, within the bound.
A program may use at most 64 MiB of HBM per device.

v0:
```python
import math

import jax
import jax.numpy as jnp
from jax import lax
from jax.sharding import PartitionSpec as P

DILATION = 8


def with_halo(block, sides, width):
    for axis, dim in sides:
        count = lax.axis_size(axis)
        forward = [(i, i + 1) for i in range(count - 1)]
        backward = [(target, source) for source, target in forward]
        low = lax.ppermute(
            lax.slice_in_dim(block, block.shape[dim] - width, None, axis=dim), axis, forward
        )
        high = lax.ppermute(lax.slice_in_dim(block, 0, width, axis=dim), axis, backward)
        block = jnp.concatenate([low, block, high], axis=dim)
    return block


def dilated(padded, conv_weight, out_rows, out_cols):
    summed = jnp.zeros((conv_weight.shape[1], out_rows, out_cols), jnp.float32)
    for tap_row in range(3):
        for tap_col in range(3):
            window = padded[
                :,
                tap_row * DILATION : tap_row * DILATION + out_rows,
                tap_col * DILATION : tap_col * DILATION + out_cols,
            ]
            summed = summed + jnp.einsum(
                "oc,crw->orw",
                conv_weight[3 * tap_row + tap_col],
                window,
                preferred_element_type=jnp.float32,
            )
    return summed


def transposed(padded, conv_weight, out_rows, out_cols):
    summed = jnp.zeros((conv_weight.shape[2], out_rows, out_cols), jnp.float32)
    for tap_row in range(3):
        for tap_col in range(3):
            first = (2 - tap_row) * DILATION
            second = (2 - tap_col) * DILATION
            window = padded[:, first : first + out_rows, second : second + out_cols]
            summed = summed + jnp.einsum(
                "oc,orw->crw",
                conv_weight[3 * tap_row + tap_col],
                window,
                preferred_element_type=jnp.float32,
            )
    return summed


def weight_grad(own_grad, padded, out_rows, out_cols, offset):
    result = []
    for tap_row in range(3):
        for tap_col in range(3):
            first = offset + tap_row * DILATION
            second = offset + tap_col * DILATION
            window = padded[:, first : first + out_rows, second : second + out_cols]
            result.append(
                jnp.einsum("orw,crw->oc", own_grad, window, preferred_element_type=jnp.float32)
            )
    return jnp.stack(result)


def head_grads(
    act_pad, upstream, conv_weight, norm_gain, norm_shift, proj_weight, out_rows, out_cols
):
    conv_out = dilated(act_pad, conv_weight, out_rows, out_cols)
    normed = norm_gain[:, None, None] * conv_out + norm_shift[:, None, None]
    sigma = jax.nn.sigmoid(normed)
    hidden = (normed * sigma).astype(jnp.bfloat16)
    back = jnp.einsum("oc,orw->crw", proj_weight, upstream, preferred_element_type=jnp.float32)
    normed_grad = back * sigma * (1.0 + normed * (1.0 - sigma))
    conv_out_grad = (norm_gain[:, None, None] * normed_grad).astype(jnp.bfloat16)
    return (conv_out_grad, hidden, normed_grad, conv_out)


def shards(pair_in, row_feat, col_feat, cotangent, conv_weight, norm_gain, norm_shift, proj_weight):
    channels, row_count, col_count = pair_in.shape
    width_bins = row_count * lax.axis_size("row")
    row_full = lax.all_gather(row_feat, "col", axis=0, tiled=True)
    col_full = lax.all_gather(col_feat, "row", axis=0, tiled=True)
    pre = (
        pair_in.astype(jnp.float32)
        + row_full.astype(jnp.float32)[:, :, None]
        + col_full.astype(jnp.float32)[:, None, :]
    )
    active = jnp.maximum(pre, 0.0).astype(jnp.bfloat16)
    act_pad = with_halo(active, (("row", 1), ("col", 2)), DILATION)
    conv_out_grad, hidden, normed_grad, conv_out = head_grads(
        act_pad, cotangent, conv_weight, norm_gain, norm_shift, proj_weight, row_count, col_count
    )
    grad_pad = with_halo(conv_out_grad, (("row", 1), ("col", 2)), DILATION)
    offset = 0
    proj_part = jnp.einsum("orw,crw->oc", cotangent, hidden, preferred_element_type=jnp.float32)
    gain_part = jnp.sum(normed_grad * conv_out, axis=(1, 2))
    shift_part = jnp.sum(normed_grad, axis=(1, 2))
    own_grad = grad_pad[:, DILATION : DILATION + row_count, DILATION : DILATION + col_count]
    conv_part = weight_grad(own_grad, act_pad, row_count, col_count, offset)
    conv_sum, proj_sum, gain_sum, shift_sum = lax.psum(
        (conv_part, proj_part, gain_part, shift_part), ("row", "col")
    )
    act_grad = transposed(grad_pad, conv_weight, row_count, col_count)
    pre_grad = jnp.where(pre > 0, act_grad, 0.0)
    pair_grad = (cotangent.astype(jnp.float32) + pre_grad).astype(jnp.bfloat16)
    root = math.sqrt(width_bins)
    row_grad = (
        lax.psum_scatter(jnp.sum(pre_grad, axis=2), "col", scatter_dimension=0, tiled=True) / root
    )
    col_grad = (
        lax.psum_scatter(jnp.sum(pre_grad, axis=1), "row", scatter_dimension=0, tiled=True) / root
    )
    return (
        pair_grad,
        row_grad,
        col_grad,
        conv_sum / width_bins,
        proj_sum / width_bins,
        gain_sum / width_bins,
        shift_sum / width_bins,
    )


def solution(mesh):
    return jax.shard_map(
        shards,
        mesh=mesh,
        in_specs=(
            P(None, "row", "col"),
            P("col", "row"),
            P("row", "col"),
            P(None, "row", "col"),
            P(),
            P(),
            P(),
            P(),
        ),
        out_specs=(P(None, "row", "col"), P("col", "row"), P("row", "col"), P(), P(), P(), P()),
        check_vma=False,
    )
```

profile of v0, /device:TPU:1, one launch (start us, length us, event | category | flops | bytes accessed | tf_op | source)
XLA Modules:
  0.0 603.6 jit_solution(5019221373790295232)
XLA Ops:
  7.2 38.4 %all-gather = bf16[32,2,128]{2,1,0:T(2,128)(2,1)S(1)} all-gather(bf16[1,2,128]{2,1,0:T(2,128)(2,1)} %bitcast.152), channel_id=1, replica_groups=mesh['row'=32,'col'=8] {'row'}, dimensions={0}, use_global_device_ids=true | all-gather | bytes 16896 | tf_op jit(solution)/shard_map/all_gather | solution.py:88
  45.7 25.5 %all_gather.6 = bf16[64,32]{1,0:T(8,128)(2,1)S(1)} all-gather(bf16[8,32]{1,0:T(8,128)(2,1)} %param.9), channel_id=1, replica_groups=mesh['row'=32,'col'=8] {'col'}, dimensions={0}, use_global_device_ids=true | all-gather | bytes 4608 | tf_op jit(solution)/shard_map/all_gather | solution.py:87
  71.3 1.4 maximum_convert_fusion
  72.7 4.4 collective-permute-start
  77.1 3.6 collective-permute-start.1
  80.7 1.2 fusion.74
  82.0 0.6 dynamic-slice
  82.6 0.6 dynamic-slice.2
  84.6 0.4 fusion.113
  85.2 2.8 collective-permute-start.2
  88.3 1.3 collective-permute-start.3
  89.6 1.3 fusion.62
  90.9 1.3 fusion.63
  92.1 0.4 copy.90
  92.5 2.4 collective-permute-done.3
  94.9 1.2 copy.92
  96.1 2.6 maximum_maximum_fusion
  98.7 0.4 fusion.56
  99.1 0.4 fusion.45
  100.1 0.6 copy-done.4
  100.7 0.3 copy-done.6
  101.0 0.4 fusion.6
  101.4 0.8 copy-done.5
  102.2 0.4 fusion.3
  102.7 0.6 copy-done.12
  103.3 0.5 convolution_bitcast_fusion
  103.8 0.8 fusion.110
  104.7 0.3 fusion.24
  105.0 0.7 fusion.114
  105.7 1.3 fusion.72
  107.1 80.9 %all-reduce.2 = (f32[64,64]{0,1:T(8,128)S(1)}, f32[64]{0:T(128)S(1)}, f32[64]{0:T(128)S(1)}) all-reduce(f32[64,64]{0,1:T(8,128)S(1)} %convolution_bitcast_fusion, f32[64]{0:T(128)S(1)} %get-tuple-element.36, f32[64]{0:T(128)S(1)} %get-tuple-element.35), channel_id=1, replica_groups=mesh['row'=32,'col'=8] {'row','col'}, use_global_device_ids=true, to_apply=%region_5.0 | all-reduce | flops 4224 | bytes 33792 | tf_op jit(solution)/shard_map/psum | solution.py:106
  188.0 0.7 copy.109
  189.0 0.4 fusion.22
  189.3 0.7 copy-done.2
  190.7 0.4 fusion.19
  191.0 0.3 fusion.18
  191.6 0.4 fusion.16
  192.0 0.7 copy-done.16
  192.8 2.7 collective-permute-start.5
  195.5 2.8 collective-permute-start.4
  198.4 0.5 broadcast_multiply_fusion.2
  198.9 234.4 %all-reduce.5.cloned.1.call-done = f32[9,64,64]{2,1,0:T(8,128)} async-done(((f32[9,64,64]{2,1,0:T(8,128)}), f32[9,64,64]{2,1,0:T(8,128)}) %all-reduce.5.cloned.1.call-update) | async-done | bytes 147472 | tf_op jit(solution)/shard_map/psum | solution.py:106
  433.2 1.7 broadcast_multiply_fusion
  435.0 0.4 fusion.112
  435.7 1.3 collective-permute-start.6
  437.3 4.2 collective-permute-start.7
  441.4 0.3 fusion.26
  441.8 0.3 fusion.30
  442.1 1.2 copy.94
  443.3 1.2 copy.98
  444.5 2.8 pad_maximum_fusion.1
  447.3 0.3 fusion.41
  447.7 0.3 fusion.34
  448.0 0.4 fusion.39
  448.4 0.4 fusion.36
  448.8 0.4 copy-done.3
  449.2 0.5 fusion.14
  449.8 0.5 copy-done.7
  450.4 1.1 fusion.111
  451.6 1.1 copy.108
  452.8 33.8 %all-reduce = f32[64,32]{1,0:T(8,128)S(1)} all-reduce(f32[64,32]{1,0:T(8,128)S(1)} %copy.106), channel_id=2, replica_groups=mesh['row'=32,'col'=8] {'col'}, use_global_device_ids=true, to_apply=%region_1.0.clone | all-reduce | flops 2048 | bytes 16384
  486.6 109.0 %all-reduce.1 = f32[64,128]{1,0:T(8,128)S(1)} all-reduce(f32[64,128]{1,0:T(8,128)S(1)} %get-tuple-element.37), channel_id=3, replica_groups=mesh['row'=32,'col'=8] {'row'}, use_global_device_ids=true, to_apply=%region_3.0.clone | all-reduce | flops 8192 | bytes 65536
  595.6 0.6 dynamic-slice_multiply_fusion
  596.2 0.6 dynamic-slice_multiply_fusion.1
  (67 shorter events, 3.5 us)
Async XLA Ops:
  7.2 96.7 %copy-start = (bf16[64,64]{1,0:T(8,128)(2,1)S(1)}, bf16[64,64]{1,0:T(8,128)(2,1)}, u32[]{:S(2)}) copy-start(bf16[64,64]{1,0:T(8,128)(2,1)} %param.15) | copy-start | bytes 24580
  7.2 73.6 %copy-start.10 = (bf16[9,64,64]{2,1,0:T(8,128)(2,1)S(1)}, bf16[9,64,64]{2,1,0:T(8,128)(2,1)}, u32[]{:S(2)}) copy-start(bf16[9,64,64]{2,1,0:T(8,128)(2,1)} %param.12) | copy-start | bytes 221188
  7.2 426.0 %all-reduce.5.cloned.1.call-start = ((), (), s32[]{:S(2)}) async-start(), calls=%async_computation | async-start | bytes 589824 | tf_op jit(solution)/shard_map/psum | solution.py:106
  45.7 27.0 %copy-start.14 = (f32[64,128]{1,0:T(8,128)}, f32[64,128]{1,0:T(8,128)S(1)}, u32[]{:S(2)}) copy-start(f32[64,128]{1,0:T(8,128)S(1)} %convert) | copy-start | bytes 98308
  71.2 1.5 copy-start.17
  71.2 10.7 %copy-start.23 = (u32[256]{0:T(256)S(1)}, u32[256]{0:T(256)}, u32[]{:S(2)}) copy-start(u32[256]{0:T(256)} %constant.21) | copy-start | bytes 3076
  71.3 11.3 %copy-start.22 = (u32[256]{0:T(256)S(1)}, u32[256]{0:T(256)}, u32[]{:S(2)}) copy-start(u32[256]{0:T(256)} %constant.25) | copy-start | bytes 3076
  72.7 11.7 %collective-permute-start = (bf16[64,8,128]{2,0,1:T(8,128)(2,1)S(1)}, bf16[64,8,128]{2,0,1:T(8,128)(2,1)S(1)}, u32[]{:S(2)}, u32[]{:S(2)}) collective-permute-start(bf16[64,8,128]{2,0,1:T(8,128)(2,1)S(1)} %get-tuple-element.54), channel_id=1, source_target_pairs={{0,8},{8,16},{16,24},{24,32},{32,40},{40,48},{48,56},{56,64},{64,7... | collective-permute-start | bytes 393224 | tf_op jit(solution)/shard_map/ppermute | solution.py:16
  77.1 7.3 %collective-permute-start.1 = (bf16[64,8,128]{2,0,1:T(8,128)(2,1)S(1)}, bf16[64,8,128]{2,0,1:T(8,128)(2,1)S(1)}, u32[]{:S(2)}, u32[]{:S(2)}) collective-permute-start(bf16[64,8,128]{2,0,1:T(8,128)(2,1)S(1)} %get-tuple-element.55), channel_id=1, source_target_pairs={{8,0},{16,8},{24,16},{32,24},{40,32},{48,40},{56,48},{64,56},{72,6... | collective-permute-start | bytes 393224 | tf_op jit(solution)/shard_map/ppermute | solution.py:19
  84.5 11.6 %copy-start.8 = (bf16[64,8,128]{2,0,1:T(8,128)(2,1)}, bf16[64,8,128]{2,0,1:T(8,128)(2,1)S(1)}, u32[]{:S(2)}) copy-start(bf16[64,8,128]{2,0,1:T(8,128)(2,1)S(1)} %collective-permute-done) | copy-start | bytes 393220
  85.2 6.9 %collective-permute-start.2 = (bf16[64,48,8]{0,2,1:T(8,128)(2,1)S(1)}, bf16[64,48,8]{0,2,1:T(8,128)(2,1)S(1)}, u32[]{:S(2)}, u32[]{:S(2)}) collective-permute-start(bf16[64,48,8]{0,2,1:T(8,128)(2,1)S(1)} %copy.89), channel_id=1, source_target_pairs={{0,1},{1,2},{2,3},{3,4},{4,5},{5,6},{6,7},{8,9},{9,10},{10,11},{11... | collective-permute-start | bytes 147464 | tf_op jit(solution)/shard_map/ppermute | solution.py:16
  88.3 6.6 %collective-permute-start.3 = (bf16[64,48,8]{0,2,1:T(8,128)(2,1)S(1)}, bf16[64,48,8]{0,2,1:T(8,128)(2,1)S(1)}, u32[]{:S(2)}, u32[]{:S(2)}) collective-permute-start(bf16[64,48,8]{0,2,1:T(8,128)(2,1)S(1)} %copy.91), channel_id=1, source_target_pairs={{1,0},{2,1},{3,2},{4,3},{5,4},{6,5},{7,6},{9,8},{10,9},{11,10},{12... | collective-permute-start | bytes 147464 | tf_op jit(solution)/shard_map/ppermute | solution.py:19
  98.7 6.0 copy-start.1
  99.5 1.2 copy-start.4
  99.5 1.5 copy-start.6
  101.0 1.2 copy-start.5
  102.2 1.0 copy-start.12
  102.2 1.0 copy-start.20
  102.2 1.0 copy-start.21
  104.7 1.1 copy-start.11
  104.7 84.0 %copy-start.9 = (bf16[64,8,128]{2,0,1:T(8,128)(2,1)S(1)}, bf16[64,8,128]{2,0,1:T(8,128)(2,1)}, u32[]{:S(2)}) copy-start(bf16[64,8,128]{2,0,1:T(8,128)(2,1)} %copy-done.8) | copy-start | bytes 393220
  188.7 1.4 copy-start.2
  191.3 4.2 copy-start.19
  192.0 0.7 copy-start.16
  192.8 242.2 %collective-permute-start.5 = (bf16[64,8,128]{2,0,1:T(8,128)(2,1)}, bf16[64,8,128]{2,0,1:T(8,128)(2,1)S(1)}, u32[]{:S(2)}, u32[]{:S(2)}) collective-permute-start(bf16[64,8,128]{2,0,1:T(8,128)(2,1)} %get-tuple-element.53), channel_id=1, source_target_pairs={{8,0},{16,8},{24,16},{32,24},{40,32},{48,40},{56,48},{64,56},{72,6... | collective-permute-start | bytes 393224 | tf_op jit(solution)/shard_map/ppermute | solution.py:19
  195.5 239.4 %collective-permute-start.4 = (bf16[64,8,128]{2,0,1:T(8,128)(2,1)S(1)}, bf16[64,8,128]{2,0,1:T(8,128)(2,1)S(1)}, u32[]{:S(2)}, u32[]{:S(2)}) collective-permute-start(bf16[64,8,128]{2,0,1:T(8,128)(2,1)S(1)} %copy-done.19), channel_id=1, source_target_pairs={{0,8},{8,16},{16,24},{24,32},{32,40},{40,48},{48,56},{56,64},{64,7... | collective-permute-start | bytes 393224 | tf_op jit(solution)/shard_map/ppermute | solution.py:16
  435.7 6.4 %collective-permute-start.6 = (bf16[64,48,8]{0,2,1:T(8,128)(2,1)S(1)}, bf16[64,48,8]{0,2,1:T(8,128)(2,1)S(1)}, u32[]{:S(2)}, u32[]{:S(2)}) collective-permute-start(bf16[64,48,8]{0,2,1:T(8,128)(2,1)S(1)} %copy.93), channel_id=1, source_target_pairs={{1,0},{2,1},{3,2},{4,3},{5,4},{6,5},{7,6},{9,8},{10,9},{11,10},{12... | collective-permute-start | bytes 147464 | tf_op jit(solution)/shard_map/ppermute | solution.py:19
  437.3 6.1 %collective-permute-start.7 = (bf16[64,48,8]{0,2,1:T(8,128)(2,1)S(1)}, bf16[64,48,8]{0,2,1:T(8,128)(2,1)S(1)}, u32[]{:S(2)}, u32[]{:S(2)}) collective-permute-start(bf16[64,48,8]{0,2,1:T(8,128)(2,1)S(1)} %copy.97), channel_id=1, source_target_pairs={{0,1},{1,2},{2,3},{3,4},{4,5},{5,6},{6,7},{8,9},{9,10},{10,11},{11... | collective-permute-start | bytes 147464 | tf_op jit(solution)/shard_map/ppermute | solution.py:16
  448.0 1.2 copy-start.3
  449.2 1.0 copy-start.7
  449.2 1.2 copy-start.13
  449.2 1.2 copy-start.15
  449.2 1.2 copy-start.18
Sparse Core Ops, SparseCore 0:
  192.9 240.2 all-reduce.4
where the time goes:
time: 609 us; the launch traced here: 604 us
  blocking collectives  288 us (47%)
  waiting for transfers between devices  237 us (39%)
  starting transfers between devices  23.1 us (4%)
  between operations  15.8 us (3%)
  matrix products  15.1 us (2%)
  local copies, waits for them, and re-layouts  14.7 us (2%)
  other arithmetic  10.4 us (2%)
    psum x1, waiting for transfers between devices, shards(): lax.psum((conv_part, proj_part, gain_part, shift_part), ('row', 'col'))  234 us
    unnamed x2, blocking collectives  143 us
    psum x1, blocking collectives, shards(): lax.psum((conv_part, proj_part, gain_part, shift_part), ('row', 'col'))  80.9 us
    all_gather x1, blocking collectives, shards(): col_full = lax.all_gather(col_feat, 'row', axis=0, tiled=True)  38.4 us
    all_gather x1, blocking collectives, shards(): row_full = lax.all_gather(row_feat, 'col', axis=0, tiled=True)  25.5 us
    ppermute x4, starting transfers between devices, with_halo(): lax.ppermute(lax.slice_in_dim(block, block.shape[dim] - width, None, axis...  14.2 us
  transfers between devices with their start and end apart: 9, of which 2 were waited for; matrix products, arithmetic and copies ran while one was open for 2% of the time, Pallas kernels for 0%

commit v1 on v0

v1 whole, which is shorter than its diff:
```python
import functools
import math

import jax
import jax.numpy as jnp
from jax import lax
from jax.experimental import pallas as pl
from jax.experimental.pallas import tpu as pltpu
from jax.sharding import PartitionSpec as P

C = 64
D = 8
TR = 32
TC = 128
PR = TR + 2 * D
LANES = PR * TC
OWN = D * TC
TILE = TR * TC
F32 = jnp.float32
BF16 = jnp.bfloat16
MESH = pl.DeviceIdType.MESH


def dot(a, b):
    return lax.dot_general(a, b, (((1,), (0,)), ((), ())), preferred_element_type=F32)


def dot_nt(a, b):
    return lax.dot_general(a, b, (((1,), (1,)), ((), ())), preferred_element_type=F32)


def kernel(
    nr,
    nc,
    pair_ref,
    rowf_ref,
    colf_ref,
    cot_ref,
    w_ref,
    gain_ref,
    shift_ref,
    proj_ref,
    pg_ref,
    rowg_ref,
    colg_ref,
    convg_ref,
    projg_ref,
    gaing_ref,
    shiftg_ref,
    xs,
    cs,
    wf,
    wd,
    gainb,
    shiftb,
    rf,
    cf,
    cfull,
    s2,
    c2,
    pkl,
    pkr,
    hl,
    hr,
    cv,
    bk,
    gz,
    g2,
    qkl,
    qkr,
    kl,
    kr,
    gacc,
    sacc,
    wacc,
    rs_send,
    rs_recv,
    zb,
    ag,
    cacc,
    racc,
    cgs,
    cgr,
    rgs,
    rgr,
    feat_sems,
    halo_send,
    halo_recv,
    grad_send,
    grad_recv,
    red_sems,
    out_sems,
):
    row = lax.axis_index("row")
    col = lax.axis_index("col")
    nz = nr // 4
    na = 4 * nc
    cr = 256 // na
    cpr = C // nr
    cpc = C // nc
    zi = row // 4
    ai = lax.rem(row, 4) * nc + col
    up, down = lax.rem(row + nr - 1, nr), lax.rem(row + 1, nr)
    left, right = lax.rem(col + nc - 1, nc), lax.rem(col + 1, nc)
    bins = TR * nr

    def row_peer(k):
        return (lax.rem(row + k, nr), col)

    def col_peer(k):
        return (row, lax.rem(col + k, nc))

    def a_peer(k):
        idx = lax.rem(ai + k, na)
        return (zi * 4 + idx // nc, lax.rem(idx, nc))

    def z_peer(k):
        return (lax.rem(zi + k, nz) * 4 + lax.rem(row, 4), col)

    barrier = pltpu.get_barrier_semaphore()

    def greet(peer, count):
        def body(k, _):
            pl.semaphore_signal(barrier, inc=1, device_id=peer(k), device_id_type=MESH)
            return 0

        lax.fori_loop(1, count, body, 0)

    greet(row_peer, nr)
    greet(a_peer, na)
    for dr in (up, down):
        for dc in (left, right):
            pl.semaphore_signal(barrier, inc=1, device_id=(dr, dc), device_id_type=MESH)

    lane = lax.broadcasted_iota(jnp.int32, (C, TC), 1)

    rf[col] = jnp.concatenate(
        [rowf_ref[...].astype(F32), jnp.zeros((cpc, TC - TR), F32)], axis=1
    )
    cf[row] = colf_ref[...].astype(F32)
    for i in range(8):
        xs[pl.ds(i * 256, 256), :] = pair_ref[pl.ds(i * 8, 8)].astype(F32).reshape(256, TC)
        cs[pl.ds(i * 256, 256), :] = cot_ref[pl.ds(i * 8, 8)].astype(F32).reshape(256, TC)

    wf[...] = jnp.zeros_like(wf)
    for p in range(3):
        wf[pl.ds(C * p, C), :] = jnp.concatenate(
            [w_ref[3 * p], w_ref[3 * p + 1], w_ref[3 * p + 2], jnp.zeros((C, C), BF16)], axis=1
        )
    wf[pl.ds(3 * C, C), :] = jnp.concatenate(
        [jnp.zeros((C, 3 * C), BF16), proj_ref[...].astype(F32).T.astype(BF16)], axis=1
    )
    for q in range(3):
        stacked = jnp.concatenate(
            [w_ref[3 * (2 - p) + 2 - q].astype(F32).T for p in range(3)], axis=0
        )
        wd[:, pl.ds(C * q, C)] = stacked.astype(BF16)
    eye = lax.broadcasted_iota(jnp.int32, (C, C), 0) == lax.broadcasted_iota(jnp.int32, (C, C), 1)
    for src, dst in ((gain_ref, gainb), (shift_ref, shiftb)):
        column = jnp.sum(jnp.where(eye, src[...], 0.0), axis=1, keepdims=True)
        dst[...] = jnp.broadcast_to(column, (C, 2 * TC))

    for r in range(TR):
        c2[:, pl.ds(OWN + r * TC, TC)] = cs[pl.ds(r, C, stride=TR), :].astype(BF16)
    zeros = jnp.zeros((C, OWN), BF16)
    for part in (0, PR - D):
        c2[:, pl.ds(part * TC, OWN)] = zeros
        s2[pl.ds(3 * C, C), pl.ds(part * TC, OWN)] = zeros
    s2[pl.ds(3 * C, C), pl.ds(OWN, TILE)] = c2[:, pl.ds(OWN, TILE)]
    for part in (0, 1, 6, 7):
        gz[:, pl.ds(part * OWN, OWN)] = zeros

    pl.semaphore_wait(barrier, (nr - 1) + (na - 1) + 4)

    def rf_copy(k):
        return pltpu.make_async_remote_copy(
            rf.at[col], rf.at[col], feat_sems.at[0], feat_sems.at[1], col_peer(k), MESH
        )

    def cf_copy(k):
        return pltpu.make_async_remote_copy(
            cf.at[row], cf.at[row], feat_sems.at[2], feat_sems.at[3], row_peer(k), MESH
        )

    def start_all(copy, count):
        def body(k, _):
            copy(k).start()
            return 0

        lax.fori_loop(1, count, body, 0)

    def wait_bytes(ref, sem):
        pltpu.make_async_copy(ref, ref, sem).wait()

    start_all(rf_copy, nc)
    start_all(cf_copy, nr)
    wait_bytes(rf.at[pl.ds(0, nc - 1)], feat_sems.at[1])
    wait_bytes(cf.at[pl.ds(0, nr - 1)], feat_sems.at[3])

    for i in range(nr):
        cfull[pl.ds(i * cpr, cpr), :] = cf[i]
    row_full = rf[...].reshape(C, TC)
    col_full = cfull[...]

    def packed(parts, edge):
        result = jnp.zeros((C, TC), F32)
        for k, x in enumerate(parts):
            shift = (8 * k + edge) % TC
            moved = pltpu.roll(x, shift, 1) if shift else x
            result = jnp.where(lane // 8 == k, moved, result)
        return result.astype(BF16)

    for b in range(2):
        parts = []
        for k in range(16):
            r = 16 * b + k
            pre = xs[pl.ds(r, C, stride=TR), :] + row_full[:, r : r + 1] + col_full
            act = jnp.maximum(pre, 0.0)
            s2[pl.ds(C, C), pl.ds(OWN + r * TC, TC)] = act.astype(BF16)
            parts.append(act)
        pkl[b] = packed(parts, 0)
        pkr[b] = packed(parts, 8)

    def halo_copies(center_src, src_base, center_dst, lsend, rsend, lrecv, rrecv, ssem, rsem):
        plan = (
            (center_src(src_base, OWN), center_dst(OWN + TILE, OWN), (up, col)),
            (center_src(src_base + TILE - OWN, OWN), center_dst(0, OWN), (down, col)),
            (lsend, rrecv.at[pl.ds(1, 2)], (row, left)),
            (rsend, lrecv.at[pl.ds(1, 2)], (row, right)),
            (lsend.at[0], rrecv.at[3], (up, left)),
            (lsend.at[1], rrecv.at[0], (down, left)),
            (rsend.at[0], lrecv.at[3], (up, right)),
            (rsend.at[1], lrecv.at[0], (down, right)),
        )
        return [
            pltpu.make_async_remote_copy(src, dst, ssem.at[i], rsem.at[i], device, MESH)
            for i, (src, dst, device) in enumerate(plan)
        ]

    def clear_edges(center, lrecv, rrecv):
        @pl.when(row == 0)
        def _():
            center[pl.ds(C, C), pl.ds(0, OWN)] = jnp.zeros((C, OWN), BF16)
            lrecv[0] = jnp.zeros((C, TC), BF16)
            rrecv[0] = jnp.zeros((C, TC), BF16)

        @pl.when(row == nr - 1)
        def _():
            center[pl.ds(C, C), pl.ds(OWN + TILE, OWN)] = jnp.zeros((C, OWN), BF16)
            lrecv[3] = jnp.zeros((C, TC), BF16)
            rrecv[3] = jnp.zeros((C, TC), BF16)

        @pl.when(col == 0)
        def _():
            lrecv[...] = jnp.zeros_like(lrecv)

        @pl.when(col == nc - 1)
        def _():
            rrecv[...] = jnp.zeros_like(rrecv)

    def build_shifts(center, lrecv, rrecv):
        for b in range(4):
            lo = lrecv[b].astype(F32)
            hi = rrecv[b].astype(F32)
            for k in range(16):
                r = 16 * b + k - 8
                if not 0 <= r < PR:
                    continue
                x = center[pl.ds(C, C), pl.ds(r * TC, TC)].astype(F32)
                from_left = pltpu.roll(lo, (TC - 8 * k) % TC, 1) if k else lo
                from_right = pltpu.roll(hi, 120 - 8 * k, 1) if k < 15 else hi
                center[pl.ds(0, C), pl.ds(r * TC, TC)] = jnp.where(
                    lane < 8, from_left, pltpu.roll(x, 8, 1)
                ).astype(BF16)
                center[pl.ds(2 * C, C), pl.ds(r * TC, TC)] = jnp.where(
                    lane >= 120, from_right, pltpu.roll(x, 120, 1)
                ).astype(BF16)

    def center_of(ref):
        return lambda base, size: ref.at[pl.ds(C, C), pl.ds(base, size)]

    copies = halo_copies(
        center_of(s2), OWN, center_of(s2), pkl, pkr, hl, hr, halo_send, halo_recv
    )
    for copy in copies:
        copy.start()
    for copy in copies:
        copy.wait_recv()
    clear_edges(s2, hl, hr)
    build_shifts(s2, hl, hr)

    def at(i, size=256):
        return pl.ds(pl.multiple_of(i * 256, 256), size)

    def forward(i, _):
        out = dot(wf[...], s2[:, at(i)])
        cv[:, at(i + 8)] = out[:C]
        cv[:, at(i + 4)] += out[C : 2 * C]
        cv[:, at(i)] += out[2 * C : 3 * C]
        bk[:, at(i)] = out[3 * C :]
        return 0

    lax.fori_loop(0, PR // 2, forward, 0)

    gacc[...] = jnp.zeros_like(gacc)
    sacc[...] = jnp.zeros_like(sacc)

    def head(i, _):
        conv_out = cv[:, at(i + 8)]
        gain = gainb[...]
        normed = gain * conv_out + shiftb[...]
        sigma = jax.nn.sigmoid(normed)
        s2[pl.ds(3 * C, C), at(i + 4)] = (normed * sigma).astype(BF16)
        normed_grad = bk[:, at(i + 4)] * sigma * (1.0 + normed * (1.0 - sigma))
        gacc[...] += normed_grad * conv_out
        sacc[...] += normed_grad
        grad = (gain * normed_grad).astype(BF16)
        gz[:, at(i + 8)] = grad
        g2[pl.ds(C, C), at(i + 4)] = grad
        return 0

    lax.fori_loop(0, TR // 2, head, 0)

    for b in range(2):
        parts = [
            gz[:, pl.ds(2 * OWN + (16 * b + k) * TC, TC)].astype(F32) for k in range(16)
        ]
        qkl[b] = packed(parts, 0)
        qkr[b] = packed(parts, 8)
    grad_copies = halo_copies(
        lambda base, size: gz.at[:, pl.ds(base, size)],
        2 * OWN,
        center_of(g2),
        qkl,
        qkr,
        kl,
        kr,
        grad_send,
        grad_recv,
    )
    for copy in grad_copies:
        copy.start()

    wacc[...] = jnp.zeros_like(wacc)

    def weights(i, _):
        base = i * 4
        lhs = jnp.concatenate(
            [
                gz[:, at(base + 8, 1024)],
                gz[:, at(base + 4, 1024)],
                gz[:, at(base, 1024)],
                c2[:, at(base, 1024)],
            ],
            axis=0,
        )
        wacc[...] += dot_nt(lhs, s2[:, at(base, 1024)])
        return 0

    lax.fori_loop(0, PR // 8, weights, 0)
    wacc[pl.ds(0, C), pl.ds(3 * C, 1)] = jnp.sum(gacc[...], axis=1, keepdims=True)
    wacc[pl.ds(0, C), pl.ds(3 * C + 1, 1)] = jnp.sum(sacc[...], axis=1, keepdims=True)

    for a in range(na):
        rs_send[a] = jnp.concatenate(
            [wacc[pl.ds(a * cr, cr), pl.ds(0, TC)], wacc[pl.ds(a * cr, cr), pl.ds(TC, TC)]], axis=0
        ).astype(BF16)

    def rs_copy(k):
        idx = lax.rem(ai + k, na)
        return pltpu.make_async_remote_copy(
            rs_send.at[idx], rs_recv.at[ai], red_sems.at[0], red_sems.at[1], a_peer(k), MESH
        )

    start_all(rs_copy, na)
    rs_recv[ai] = rs_send[ai]

    for copy in grad_copies:
        copy.wait_recv()
    clear_edges(g2, kl, kr)
    build_shifts(g2, kl, kr)

    def backward(i, _):
        out = dot(wd[...], g2[:, at(i)])
        cv[:, at(i + 8)] = out[:C]
        cv[:, at(i + 4)] += out[C : 2 * C]
        cv[:, at(i)] += out[2 * C :]
        return 0

    lax.fori_loop(0, PR // 2, backward, 0)

    wait_bytes(rs_recv.at[pl.ds(0, na - 1)], red_sems.at[1])
    zb[zi] = jnp.sum(rs_recv[...].astype(F32), axis=0)

    def z_copy(k):
        return pltpu.make_async_remote_copy(
            zb.at[zi], zb.at[zi], red_sems.at[2], red_sems.at[3], z_peer(k), MESH
        )

    start_all(z_copy, nz)

    root = math.sqrt(bins)
    col_sum = jnp.zeros((C, TC), F32)
    row_sum = jnp.zeros((C, TC), F32)
    for r in range(TR):
        act_grad = cv[:, pl.ds(2 * OWN + r * TC, TC)]
        active = s2[pl.ds(C, C), pl.ds(OWN + r * TC, TC)].astype(F32)
        pre_grad = jnp.where(active > 0, act_grad, 0.0)
        col_sum += pre_grad
        row_sum = jnp.where(lane == r, jnp.sum(pre_grad, axis=1, keepdims=True), row_sum)
        xs[pl.ds(r, C, stride=TR), :] = pre_grad + cs[pl.ds(r, C, stride=TR), :]
    cacc[...] = col_sum
    for i in range(nr):
        cgs[i] = cacc[pl.ds(i * cpr, cpr), :]
    rgs[...] = row_sum.reshape(nc, cpc, TC)

    def cg_copy(k):
        idx = lax.rem(row + k, nr)
        return pltpu.make_async_remote_copy(
            cgs.at[idx], cgr.at[row], out_sems.at[0], out_sems.at[1], row_peer(k), MESH
        )

    def rg_copy(k):
        idx = lax.rem(col + k, nc)
        return pltpu.make_async_remote_copy(
            rgs.at[idx], rgr.at[col], out_sems.at[2], out_sems.at[3], col_peer(k), MESH
        )

    start_all(cg_copy, nr)
    start_all(rg_copy, nc)
    cgr[row] = cgs[row]
    rgr[col] = rgs[col]

    wait_bytes(zb.at[pl.ds(0, nz - 1)], red_sems.at[3])
    ag[ai] = (jnp.sum(zb[...], axis=0) * (1.0 / bins)).astype(BF16)

    def ag_copy(k):
        return pltpu.make_async_remote_copy(
            ag.at[ai], ag.at[ai], red_sems.at[4], red_sems.at[5], a_peer(k), MESH
        )

    start_all(ag_copy, na)

    for i in range(8):
        pg_ref[pl.ds(i * 8, 8)] = xs[pl.ds(i * 256, 256), :].reshape(8, TR, TC).astype(BF16)

    wait_bytes(cgr.at[pl.ds(0, nr - 1)], out_sems.at[1])
    wait_bytes(rgr.at[pl.ds(0, nc - 1)], out_sems.at[3])
    colg_ref[...] = jnp.sum(cgr[...], axis=0) * (1.0 / root)
    rowg_ref[...] = jnp.sum(rgr[...], axis=0)[:, :TR] * (1.0 / root)

    wait_bytes(ag.at[pl.ds(0, na - 1)], red_sems.at[5])
    total = ag[...].astype(F32)
    low = total[:, :cr].reshape(256, TC)
    high = total[:, cr:].reshape(256, TC)
    for p in range(3):
        convg_ref[3 * p] = low[C * p : C * p + C, :C]
        convg_ref[3 * p + 1] = low[C * p : C * p + C, C:]
        convg_ref[3 * p + 2] = high[C * p : C * p + C, :C]
    projg_ref[...] = high[3 * C :, C:]
    gaing_ref[...] = jnp.sum(jnp.where(eye, high[:C, C : C + 1], 0.0), axis=0, keepdims=True)
    shiftg_ref[...] = jnp.sum(jnp.where(eye, high[:C, C + 1 : C + 2], 0.0), axis=0, keepdims=True)

    for copy in copies:
        copy.wait_send()
    for copy in grad_copies:
        copy.wait_send()
    wait_bytes(rf.at[pl.ds(0, nc - 1)], feat_sems.at[0])
    wait_bytes(cf.at[pl.ds(0, nr - 1)], feat_sems.at[2])
    wait_bytes(rs_send.at[pl.ds(0, na - 1)], red_sems.at[0])
    wait_bytes(zb.at[pl.ds(0, nz - 1)], red_sems.at[2])
    wait_bytes(ag.at[pl.ds(0, na - 1)], red_sems.at[4])
    wait_bytes(cgs.at[pl.ds(0, nr - 1)], out_sems.at[0])
    wait_bytes(rgs.at[pl.ds(0, nc - 1)], out_sems.at[2])


def shards(nr, nc, pair_in, row_feat, col_feat, cotangent, conv_weight, gain, shift, proj):
    na, nz = 4 * nc, nr // 4
    cr = 256 // na
    vmem = pl.BlockSpec(memory_space=pltpu.VMEM)
    scratch = dict(
        xs=pltpu.VMEM((C * TR, TC), F32),
        cs=pltpu.VMEM((C * TR, TC), F32),
        wf=pltpu.VMEM((4 * C, 4 * C), BF16),
        wd=pltpu.VMEM((3 * C, 3 * C), BF16),
        gainb=pltpu.VMEM((C, 2 * TC), F32),
        shiftb=pltpu.VMEM((C, 2 * TC), F32),
        rf=pltpu.VMEM((nc, C // nc, TC), F32),
        cf=pltpu.VMEM((nr, C // nr, TC), F32),
        cfull=pltpu.VMEM((C, TC), F32),
        s2=pltpu.VMEM((4 * C, LANES), BF16),
        c2=pltpu.VMEM((C, LANES), BF16),
        pkl=pltpu.VMEM((2, C, TC), BF16),
        pkr=pltpu.VMEM((2, C, TC), BF16),
        hl=pltpu.VMEM((4, C, TC), BF16),
        hr=pltpu.VMEM((4, C, TC), BF16),
        cv=pltpu.VMEM((C, LANES + 2 * OWN), F32),
        bk=pltpu.VMEM((C, LANES), F32),
        gz=pltpu.VMEM((C, LANES + 2 * OWN), BF16),
        g2=pltpu.VMEM((3 * C, LANES), BF16),
        qkl=pltpu.VMEM((2, C, TC), BF16),
        qkr=pltpu.VMEM((2, C, TC), BF16),
        kl=pltpu.VMEM((4, C, TC), BF16),
        kr=pltpu.VMEM((4, C, TC), BF16),
        gacc=pltpu.VMEM((C, 2 * TC), F32),
        sacc=pltpu.VMEM((C, 2 * TC), F32),
        wacc=pltpu.VMEM((4 * C, 4 * C), F32),
        rs_send=pltpu.VMEM((na, 2 * cr, TC), BF16),
        rs_recv=pltpu.VMEM((na, 2 * cr, TC), BF16),
        zb=pltpu.VMEM((nz, 2 * cr, TC), F32),
        ag=pltpu.VMEM((na, 2 * cr, TC), BF16),
        cacc=pltpu.VMEM((C, TC), F32),
        racc=pltpu.VMEM((C, TC), F32),
        cgs=pltpu.VMEM((nr, C // nr, TC), F32),
        cgr=pltpu.VMEM((nr, C // nr, TC), F32),
        rgs=pltpu.VMEM((nc, C // nc, TC), F32),
        rgr=pltpu.VMEM((nc, C // nc, TC), F32),
        feat_sems=pltpu.SemaphoreType.DMA((4,)),
        halo_send=pltpu.SemaphoreType.DMA((8,)),
        halo_recv=pltpu.SemaphoreType.DMA((8,)),
        grad_send=pltpu.SemaphoreType.DMA((8,)),
        grad_recv=pltpu.SemaphoreType.DMA((8,)),
        red_sems=pltpu.SemaphoreType.DMA((6,)),
        out_sems=pltpu.SemaphoreType.DMA((4,)),
    )
    outs = pl.pallas_call(
        functools.partial(kernel, nr, nc),
        out_shape=(
            jax.ShapeDtypeStruct((C, TR, TC), BF16),
            jax.ShapeDtypeStruct((C // nc, TR), F32),
            jax.ShapeDtypeStruct((C // nr, TC), F32),
            jax.ShapeDtypeStruct((9, C, C), F32),
            jax.ShapeDtypeStruct((C, C), F32),
            jax.ShapeDtypeStruct((1, C), F32),
            jax.ShapeDtypeStruct((1, C), F32),
        ),
        in_specs=[vmem] * 8,
        out_specs=(vmem,) * 7,
        scratch_shapes=list(scratch.values()),
        compiler_params=pltpu.CompilerParams(
            collective_id=0, has_side_effects=True, vmem_limit_bytes=48 * 1024 * 1024
        ),
    )(
        pair_in,
        row_feat,
        col_feat,
        cotangent,
        conv_weight,
        gain.reshape(1, C),
        shift.reshape(1, C),
        proj,
    )
    return (*outs[:5], outs[5].reshape(C), outs[6].reshape(C))


def solution(mesh):
    return jax.shard_map(
        functools.partial(shards, mesh.shape["row"], mesh.shape["col"]),
        mesh=mesh,
        in_specs=(
            P(None, "row", "col"),
            P("col", "row"),
            P("row", "col"),
            P(None, "row", "col"),
            P(),
            P(),
            P(),
            P(),
        ),
        out_specs=(P(None, "row", "col"), P("col", "row"), P("row", "col"), P(), P(), P(), P()),
        check_vma=False,
    )
```

time: 609 us -> 65.6 us (0.11)
  blocking collectives: 288 us -> 0 us
  waiting for transfers between devices: 237 us -> 0 us
  Pallas kernels: 0 us -> 56 us
  starting transfers between devices: 23.1 us -> 0 us
  between operations: 15.8 us -> 0.68 us
  matrix products: 15.1 us -> 0 us
  other arithmetic: 10.4 us -> 0 us
    psum x1 -> x0, waiting for transfers between devices: 234 us -> none  [shards(): lax.psum((conv_part, proj_part, gain_part, shift_part), ('row', 'col'))]
    unnamed x2 -> x0, blocking collectives: 143 us -> none
    psum x1 -> x0, blocking collectives: 80.9 us -> none  [shards(): lax.psum((conv_part, proj_part, gain_part, shift_part), ('row', 'col'))]
    all_gather x2 -> x0, blocking collectives: 63.9 us -> none  [the longest x1 38.4 us: shards(): col_full = lax.all_gather(col_feat, 'row', axis=0, tiled=True)]
    pallas_call x0 -> x1, Pallas kernels: none -> 56 us  [shards(): pl.pallas_call(functools.partial(kernel, nr, nc), out_shape=(jax.ShapeDty...]
    ppermute x8 -> x0, starting transfers between devices: 23.1 us -> none  [the longest x4 14.2 us: with_halo(): lax.ppermute(lax.slice_in_dim(block, block.shape[dim] - width, None, axis...]
    dot_general x29 -> x0, matrix products: 15.1 us -> none  [the longest x9 5.81 us: dilated(): jnp.einsum('oc,crw->orw', conv_weight[3 * tap_row + tap_col], window, pre...]
  transfers between devices with their start and end apart: 9 -> 0, of which waited for: 2 -> 0; matrix products, arithmetic and copies ran while one was open for 2% -> 0% of each run, Pallas kernels for 0% -> 0%
where the time goes in v1:
time: 65.6 us; the launch traced here: 65.4 us
  Pallas kernels  56 us (85%)
  local copies, waits for them, and re-layouts  8.68 us (13%)
  between operations  0.68 us (1%)
    pallas_call x1, Pallas kernels, shards(): pl.pallas_call(functools.partial(kernel, nr, nc), out_shape=(jax.ShapeDty...  56 us
    unnamed x23, local copies, waits for them, and re-layouts  8.68 us

profile of v1, /device:TPU:1, one launch (start us, length us, event | category | flops | bytes accessed | tf_op | source)
XLA Modules:
  0.0 65.4 jit_solution(7198764021389558542)
XLA Ops:
  0.6 0.0 copy-start.4
  0.6 0.0 copy-start.5
  0.7 0.0 copy-start.6
  0.7 0.0 copy-start.7
  0.7 0.6 copy-done.4
  1.3 0.0 copy-done.5
  1.3 0.0 copy-done.6
  1.3 0.0 copy-done.7
  1.3 0.0 copy-start
  1.3 1.0 %copy-done = bf16[64,32,128]{2,1,0:T(8,128)(2,1)S(1)} copy-done((bf16[64,32,128]{2,1,0:T(8,128)(2,1)S(1)}, bf16[64,32,128]{2,1,0:T(8,128)(2,1)}, u32[]{:S(2)}) %copy-start) | copy-done | bytes 524312
  2.4 0.0 copy-start.1
  2.4 1.0 %copy-done.1 = bf16[64,32,128]{2,1,0:T(8,128)(2,1)S(1)} copy-done((bf16[64,32,128]{2,1,0:T(8,128)(2,1)S(1)}, bf16[64,32,128]{2,1,0:T(8,128)(2,1)}, u32[]{:S(2)}) %copy-start.1) | copy-done | bytes 524312
  3.4 0.0 copy-start.2
  3.4 0.9 %copy-done.2 = bf16[9,64,64]{2,1,0:T(8,128)(2,1)S(1)} copy-done((bf16[9,64,64]{2,1,0:T(8,128)(2,1)S(1)}, bf16[9,64,64]{2,1,0:T(8,128)(2,1)}, u32[]{:S(2)}) %copy-start.2) | copy-done | bytes 73752
  4.3 0.0 copy-start.3
  4.3 0.7 %copy-done.3 = bf16[64,64]{1,0:T(8,128)(2,1)S(1)} copy-done((bf16[64,64]{1,0:T(8,128)(2,1)S(1)}, bf16[64,64]{1,0:T(8,128)(2,1)}, u32[]{:S(2)}) %copy-start.3) | copy-done | bytes 8216
  5.1 56.0 %shard_map.135 = (bf16[64,32,128]{2,1,0:T(8,128)(2,1)S(1)}, f32[8,32]{1,0:T(8,128)S(1)}, f32[2,128]{1,0:T(2,128)S(1)}, f32[9,64,64]{2,1,0:T(8,128)S(1)}, f32[64,...) custom-call(bf16[64,32,128]{2,1,0:T(8,128)(2,1)S(1)} %copy-done, bf16[8,32]{1,0:T(8,128)(2,1)S(1)} %copy-done.4, ...), custom_call_target="tpu_custom_call" | custom-call | tf_op jit(solution)/shard_map/pallas_call | solution.py:526
  61.1 0.8 %copy.22 = bf16[64,32,128]{2,1,0:T(8,128)(2,1)} copy(bf16[64,32,128]{2,1,0:T(8,128)(2,1)S(1)} %get-tuple-element.28) | data formatting | bytes 1048576
  61.9 0.6 copy.23
  62.5 0.6 copy.24
  63.0 0.7 %copy.25 = f32[9,64,64]{2,1,0:T(8,128)} copy(f32[9,64,64]{2,1,0:T(8,128)S(1)} %get-tuple-element.31) | data formatting | bytes 294912
  63.7 0.6 copy.26
  64.3 0.5 copy.27
  64.9 0.5 copy.28
Async XLA Ops:
  0.6 0.7 %copy-start.4 = (bf16[8,32]{1,0:T(8,128)(2,1)S(1)}, bf16[8,32]{1,0:T(8,128)(2,1)}, u32[]{:S(2)}) copy-start(bf16[8,32]{1,0:T(8,128)(2,1)} %rowf_ref.1) | copy-start | bytes 1540
  0.6 0.7 %copy-start.5 = (bf16[2,128]{1,0:T(2,128)(2,1)S(1)}, bf16[2,128]{1,0:T(2,128)(2,1)}, u32[]{:S(2)}) copy-start(bf16[2,128]{1,0:T(2,128)(2,1)} %colf_ref.1) | copy-start | bytes 1540
  0.7 0.7 %copy-start.6 = (f32[64]{0:T(128)S(1)}, f32[64]{0:T(128)}, u32[]{:S(2)}) copy-start(f32[64]{0:T(128)} %param.13) | copy-start | bytes 772
  0.7 0.7 %copy-start.7 = (f32[64]{0:T(128)S(1)}, f32[64]{0:T(128)}, u32[]{:S(2)}) copy-start(f32[64]{0:T(128)} %param.14) | copy-start | bytes 772
  1.3 1.0 %copy-start = (bf16[64,32,128]{2,1,0:T(8,128)(2,1)S(1)}, bf16[64,32,128]{2,1,0:T(8,128)(2,1)}, u32[]{:S(2)}) copy-start(bf16[64,32,128]{2,1,0:T(8,128)(2,1)} %pair_ref.1) | copy-start | bytes 1572868
  2.4 1.0 %copy-start.1 = (bf16[64,32,128]{2,1,0:T(8,128)(2,1)S(1)}, bf16[64,32,128]{2,1,0:T(8,128)(2,1)}, u32[]{:S(2)}) copy-start(bf16[64,32,128]{2,1,0:T(8,128)(2,1)} %cot_ref.1) | copy-start | bytes 1572868
  3.4 0.9 %copy-start.2 = (bf16[9,64,64]{2,1,0:T(8,128)(2,1)S(1)}, bf16[9,64,64]{2,1,0:T(8,128)(2,1)}, u32[]{:S(2)}) copy-start(bf16[9,64,64]{2,1,0:T(8,128)(2,1)} %w_ref.1) | copy-start | bytes 221188
  4.3 0.7 %copy-start.3 = (bf16[64,64]{1,0:T(8,128)(2,1)S(1)}, bf16[64,64]{1,0:T(8,128)(2,1)}, u32[]{:S(2)}) copy-start(bf16[64,64]{1,0:T(8,128)(2,1)} %proj_ref.1) | copy-start | bytes 24580

commit v2 on v1

v2 whole, which is shorter than its diff:
```python
import functools
import math

import jax
import jax.numpy as jnp
from jax import lax
from jax.experimental import pallas as pl
from jax.experimental.pallas import tpu as pltpu
from jax.sharding import PartitionSpec as P

C = 64
D = 8
TR = 32
TC = 128
PR = TR + 2 * D
LANES = PR * TC
OWN = D * TC
TILE = TR * TC
F32 = jnp.float32
BF16 = jnp.bfloat16
VMEM_LIMIT = 60 * 1024 * 1024
MESH = pl.DeviceIdType.MESH


def dot(a, b):
    return lax.dot_general(a, b, (((1,), (0,)), ((), ())), preferred_element_type=F32)


def dot_nt(a, b):
    return lax.dot_general(a, b, (((1,), (1,)), ((), ())), preferred_element_type=F32)


def kernel(
    nr,
    nc,
    pair_in,
    rowf_in,
    colf_in,
    cot_in,
    w_in,
    gain_in,
    shift_in,
    proj_in,
    pg_out,
    rowg_out,
    colg_out,
    convg_out,
    projg_out,
    gaing_out,
    shiftg_out,
    pg_ref,
    rowg_ref,
    colg_ref,
    convg_ref,
    projg_ref,
    gaing_ref,
    shiftg_ref,
    pair_ref,
    rowf_ref,
    colf_ref,
    cot_ref,
    w_ref,
    gain_ref,
    shift_ref,
    proj_ref,
    xs,
    wf,
    pt,
    wd,
    gainb,
    shiftb,
    rf,
    cf,
    cfull,
    pc,
    rsend,
    csend,
    rnear,
    cnear,
    s2,
    gh,
    c2,
    pkl,
    pkr,
    hl,
    hr,
    gz,
    g2,
    qkl,
    qkr,
    kl,
    kr,
    wacc,
    rs_send,
    rs_recv,
    zb,
    ag,
    cacc,
    cgs,
    cgr,
    rgs,
    rgr,
    in_sems,
    store_sems,
    feat_sems,
    side_sems,
    halo_send,
    halo_recv,
    grad_send,
    grad_recv,
    red_sems,
    out_sems,
):
    row = lax.axis_index("row")
    col = lax.axis_index("col")
    nz = nr // 4
    na = 4 * nc
    cr = 256 // na
    cpr = C // nr
    cpc = C // nc
    zi = row // 4
    ai = lax.rem(row, 4) * nc + col
    up, down = lax.rem(row + nr - 1, nr), lax.rem(row + 1, nr)
    left, right = lax.rem(col + nc - 1, nc), lax.rem(col + 1, nc)
    bins = TR * nr

    def row_peer(k):
        return (lax.rem(row + k, nr), col)

    def col_peer(k):
        return (row, lax.rem(col + k, nc))

    def a_peer(k):
        idx = lax.rem(ai + k, na)
        return (zi * 4 + idx // nc, lax.rem(idx, nc))

    def z_peer(k):
        return (lax.rem(zi + k, nz) * 4 + lax.rem(row, 4), col)

    barrier = pltpu.get_barrier_semaphore()

    def greet(peer, count):
        def body(k, _):
            pl.semaphore_signal(barrier, inc=1, device_id=peer(k), device_id_type=MESH)
            return 0

        lax.fori_loop(1, count, body, 0)

    greet(row_peer, nr)
    greet(a_peer, na)
    for dr in (up, down):
        for dc in (left, right):
            pl.semaphore_signal(barrier, inc=1, device_id=(dr, dc), device_id_type=MESH)

    loads = [
        pltpu.make_async_copy(src, dst, in_sems.at[i])
        for i, (src, dst) in enumerate(
            (
                (rowf_in, rowf_ref),
                (colf_in, colf_ref),
                (pair_in, pair_ref),
                (cot_in, cot_ref),
                (w_in, w_ref),
                (proj_in, proj_ref),
                (gain_in, gain_ref),
                (shift_in, shift_ref),
            )
        )
    ]
    for load in loads:
        load.start()
    pending = []
    recvs = {}
    outputs = (
        (pg_ref, pg_out),
        (rowg_ref, rowg_out),
        (colg_ref, colg_out),
        (convg_ref, convg_out),
        (projg_ref, projg_out),
        (gaing_ref, gaing_out),
        (shiftg_ref, shiftg_out),
    )

    def store(first, last):
        for i in range(first, last):
            copy = pltpu.make_async_copy(*outputs[i], store_sems.at[i])
            copy.start()
            pending.append(copy.wait)


    lane = lax.broadcasted_iota(jnp.int32, (C, TC), 1)

    def packed(parts, edge):
        result = jnp.zeros((C, TC), F32)
        for k, x in enumerate(parts):
            shift = (8 * k + edge) % TC
            moved = pltpu.roll(x, shift, 1) if shift else x
            result = jnp.where(lane // 8 == k, moved, result)
        return result.astype(BF16)

    def halo_copies(center, base, target, lsend, rsend, lrecv, rrecv, ssem, rsem):
        plan = (
            (lsend.at[0], rrecv.at[3], (up, left)),
            (lsend.at[1], rrecv.at[0], (down, left)),
            (rsend.at[0], lrecv.at[3], (up, right)),
            (rsend.at[1], lrecv.at[0], (down, right)),
            (lsend, rrecv.at[pl.ds(1, 2)], (row, left)),
            (rsend, lrecv.at[pl.ds(1, 2)], (row, right)),
            (
                center.at[pl.ds(0, C), pl.ds(base, OWN)],
                target.at[pl.ds(0, C), pl.ds(OWN + TILE, OWN)],
                (up, col),
            ),
            (
                center.at[pl.ds(0, C), pl.ds(base + TILE - OWN, OWN)],
                target.at[pl.ds(0, C), pl.ds(0, OWN)],
                (down, col),
            ),
        )
        return [
            pltpu.make_async_remote_copy(src, dst, ssem.at[i], rsem.at[i], device, MESH)
            for i, (src, dst, device) in enumerate(plan)
        ]

    def clear_edges(lrecv, rrecv):
        @pl.when(row == 0)
        def _():
            lrecv[0] = jnp.zeros((C, TC), BF16)
            rrecv[0] = jnp.zeros((C, TC), BF16)

        @pl.when(row == nr - 1)
        def _():
            lrecv[3] = jnp.zeros((C, TC), BF16)
            rrecv[3] = jnp.zeros((C, TC), BF16)

        @pl.when(col == 0)
        def _():
            lrecv[...] = jnp.zeros_like(lrecv)

        @pl.when(col == nc - 1)
        def _():
            rrecv[...] = jnp.zeros_like(rrecv)

    def set_edges(ref, lrecv, rrecv):
        for b in range(4):
            lo = lrecv[b].astype(F32)
            hi = rrecv[b].astype(F32)
            for k in range(16):
                r = 16 * b + k - 8
                if not 0 <= r < PR:
                    continue
                from_left = pltpu.roll(lo, (TC - 8 * k) % TC, 1) if k else lo
                from_right = pltpu.roll(hi, 120 - 8 * k, 1) if k < 15 else hi
                at_left = ref.at[pl.ds(0, C), pl.ds(r * TC, TC)]
                at_right = ref.at[pl.ds(2 * C, C), pl.ds(r * TC, TC)]
                at_left[...] = jnp.where(
                    lane < 8, from_left, at_left[...].astype(F32)
                ).astype(BF16)
                at_right[...] = jnp.where(
                    lane >= 120, from_right, at_right[...].astype(F32)
                ).astype(BF16)

    for i in range(3):
        loads[i].wait()
    rf[col] = jnp.concatenate(
        [rowf_ref[...].astype(F32), jnp.zeros((cpc, TC - TR), F32)], axis=1
    )
    cf[row] = colf_ref[...].astype(F32)
    for i in range(8):
        xs[pl.ds(i * 256, 256), :] = pair_ref[pl.ds(i * 8, 8)].astype(F32).reshape(256, TC)
    for b in range(2):
        parts = []
        for k in range(16):
            r = 16 * b + k
            x = xs[pl.ds(r, C, stride=TR), :]
            pc[:, pl.ds(OWN + r * TC, TC)] = x.astype(BF16)
            parts.append(x)
        pkl[b] = packed(parts, 0)
        pkr[b] = packed(parts, 8)

    pl.semaphore_wait(barrier, (nr - 1) + (na - 1) + 4)

    def rf_copy(k):
        return pltpu.make_async_remote_copy(
            rf.at[col], rf.at[col], feat_sems.at[0], feat_sems.at[1], col_peer(k), MESH
        )

    def cf_copy(k):
        return pltpu.make_async_remote_copy(
            cf.at[row], cf.at[row], feat_sems.at[2], feat_sems.at[3], row_peer(k), MESH
        )

    def start_all(copy, count):
        def body(k, _):
            copy(k).start()
            return 0

        lax.fori_loop(1, count, body, 0)

    def wait_bytes(ref, sem):
        pltpu.make_async_copy(ref, ref, sem).wait()

    def wait_later(ref, send_sem, recv_sem, name):
        pending.append(lambda: wait_bytes(ref, send_sem))
        recvs[name] = lambda: wait_bytes(ref, recv_sem)

    def arrived(name):
        recvs.pop(name)()

    start_all(rf_copy, nc)
    start_all(cf_copy, nr)
    wait_later(rf.at[pl.ds(0, nc - 1)], feat_sems.at[0], feat_sems.at[1], "rf")
    wait_later(cf.at[pl.ds(0, nr - 1)], feat_sems.at[2], feat_sems.at[3], "cf")
    copies = halo_copies(pc, OWN, pc, pkl, pkr, hl, hr, halo_send, halo_recv)
    for i, copy in enumerate(copies):
        copy.start()
        pending.append(copy.wait_send)
        recvs[f"halo{i}"] = copy.wait_recv

    for i in range(3, 8):
        loads[i].wait()
    for i in range(8):
        xs[pl.ds(i * 256, 256), :] = cot_ref[pl.ds(i * 8, 8)].astype(F32).reshape(256, TC)
    for r in range(TR):
        c2[:, pl.ds(OWN + r * TC, TC)] = xs[pl.ds(r, C, stride=TR), :].astype(BF16)
    zeros = jnp.zeros((C, OWN), BF16)
    for part in (0, PR - D):
        c2[:, pl.ds(part * TC, OWN)] = zeros
        s2[pl.ds(3 * C, C), pl.ds(part * TC, OWN)] = zeros
    for part in (0, 1, 6, 7):
        gz[:, pl.ds(part * OWN, OWN)] = zeros
    for p in range(3):
        wf[p] = jnp.concatenate([w_ref[3 * p + q] for q in range(3)], axis=1)
        wd[p] = jnp.concatenate(
            [w_ref[3 * (2 - p) + 2 - q].astype(F32).T for q in range(3)], axis=1
        ).astype(BF16)
    pt[...] = proj_ref[...].astype(F32).T.astype(BF16)
    eye = lax.broadcasted_iota(jnp.int32, (C, C), 0) == lax.broadcasted_iota(jnp.int32, (C, C), 1)
    for src, dst in ((gain_ref, gainb), (shift_ref, shiftb)):
        column = jnp.sum(jnp.where(eye, src[...], 0.0), axis=1, keepdims=True)
        dst[...] = jnp.broadcast_to(column, (C, 2 * TC))
    arrived("rf")
    arrived("cf")

    for i in range(nr):
        cfull[pl.ds(i * cpr, cpr), :] = cf[i]
    row_full = rf[...].reshape(C, TC)
    col_full = cfull[...]
    rsend[...] = row_full.astype(BF16)
    csend[...] = col_full.astype(BF16)
    side_copies = [
        pltpu.make_async_remote_copy(
            src, dst, side_sems.at[2 * i], side_sems.at[2 * i + 1], device, MESH
        )
        for i, (src, dst, device) in enumerate(
            (
                (csend, cnear.at[1], (row, left)),
                (csend, cnear.at[0], (row, right)),
                (rsend, rnear.at[1], (up, col)),
                (rsend, rnear.at[0], (down, col)),
            )
        )
    ]
    for i, copy in enumerate(side_copies):
        copy.start()
        pending.append(copy.wait_send)
        recvs[f"side{i}"] = copy.wait_recv

    def activate(r, rows, at):
        pre = pc[:, pl.ds(r * TC, TC)].astype(F32) + rows[:, at : at + 1] + col_full
        return jnp.maximum(pre, 0.0)

    def place(ref, r, x):
        ref[pl.ds(0, C), pl.ds(r * TC, TC)] = pltpu.roll(x, 8, 1).astype(BF16)
        ref[pl.ds(C, C), pl.ds(r * TC, TC)] = x.astype(BF16)
        ref[pl.ds(2 * C, C), pl.ds(r * TC, TC)] = pltpu.roll(x, 120, 1).astype(BF16)

    for r in range(TR):
        place(s2, D + r, activate(D + r, row_full, r))
    for i in range(4):
        arrived(f"side{i}")
    for i in range(8):
        arrived(f"halo{i}")
    above, below = rnear[0].astype(F32), rnear[1].astype(F32)
    for r in range(D):
        top = activate(r, above, TR - D + r)
        place(s2, r, jnp.where(row > 0, top, 0.0))
        bottom = activate(D + TR + r, below, r)
        place(s2, D + TR + r, jnp.where(row < nr - 1, bottom, 0.0))

    def spread(first, divide):
        source = lax.broadcasted_iota(jnp.int32, (TC, TC), 0)
        target = lax.broadcasted_iota(jnp.int32, (TC, TC), 1)
        wanted = target // 8 if divide else target % 8
        return (source == first + wanted).astype(BF16)

    per_row = (
        dot(rnear[0], spread(TR - 16, True)),
        dot(rsend[...], spread(0, True)),
        dot(rsend[...], spread(16, True)),
        dot(rnear[1], spread(0, True)),
    )
    per_col = (dot(cnear[0], spread(TC - 8, False)), dot(cnear[1], spread(0, False)))
    for b in range(4):
        for buffer, feature in ((hl, per_col[0]), (hr, per_col[1])):
            pre = buffer[b].astype(F32) + per_row[b] + feature
            buffer[b] = jnp.maximum(pre, 0.0).astype(BF16)
    clear_edges(hl, hr)
    set_edges(s2, hl, hr)

    gain, shift = gainb[...], shiftb[...]
    gain_sum = jnp.zeros((C, TC), F32)
    shift_sum = jnp.zeros((C, TC), F32)
    for i in range(TR // 2):
        here = pl.ds(OWN + i * 256, 256)
        conv_out = sum(
            dot(wf[p], s2[pl.ds(0, 3 * C), pl.ds(p * OWN + i * 256, 256)]) for p in range(3)
        )
        back = dot(pt[...], c2[:, here])
        normed = gain * conv_out + shift
        sigma = jax.nn.sigmoid(normed)
        s2[pl.ds(3 * C, C), here] = (normed * sigma).astype(BF16)
        normed_grad = back * sigma * (1.0 + normed * (1.0 - sigma))
        product = normed_grad * conv_out
        gain_sum += product[:, :TC] + product[:, TC:]
        shift_sum += normed_grad[:, :TC] + normed_grad[:, TC:]
        gz[:, pl.ds(2 * OWN + i * 256, 256)] = (gain * normed_grad).astype(BF16)
    for b in range(2):
        parts = [
            gz[:, pl.ds(2 * OWN + (16 * b + k) * TC, TC)].astype(F32) for k in range(16)
        ]
        qkl[b] = packed(parts, 0)
        qkr[b] = packed(parts, 8)
    grad_copies = halo_copies(gz, 2 * OWN, gh, qkl, qkr, kl, kr, grad_send, grad_recv)
    for i, copy in enumerate(grad_copies):
        copy.start()
        pending.append(copy.wait_send)
        recvs[f"grad{i}"] = copy.wait_recv

    total = jnp.zeros((4 * C, 4 * C), F32)
    step = 1024
    for base in range(0, LANES, step):
        lhs = jnp.concatenate(
            [
                gz[:, pl.ds(base + 2 * OWN, step)],
                gz[:, pl.ds(base + OWN, step)],
                gz[:, pl.ds(base, step)],
                c2[:, pl.ds(base, step)],
            ],
            axis=0,
        )
        total += dot_nt(lhs, s2[:, pl.ds(base, step)])
    wacc[...] = total
    wacc[pl.ds(0, C), pl.ds(3 * C, 1)] = jnp.sum(gain_sum, axis=1, keepdims=True)
    wacc[pl.ds(0, C), pl.ds(3 * C + 1, 1)] = jnp.sum(shift_sum, axis=1, keepdims=True)

    for a in range(na):
        rs_send[a] = jnp.concatenate(
            [wacc[pl.ds(a * cr, cr), pl.ds(0, TC)], wacc[pl.ds(a * cr, cr), pl.ds(TC, TC)]], axis=0
        ).astype(BF16)

    def rs_copy(k):
        idx = lax.rem(ai + k, na)
        return pltpu.make_async_remote_copy(
            rs_send.at[idx], rs_recv.at[ai], red_sems.at[0], red_sems.at[1], a_peer(k), MESH
        )

    start_all(rs_copy, na)
    wait_later(rs_send.at[pl.ds(0, na - 1)], red_sems.at[0], red_sems.at[1], "rs")
    rs_recv[ai] = rs_send[ai]

    for r in range(TR):
        place(g2, D + r, gz[:, pl.ds(2 * OWN + r * TC, TC)].astype(F32))
    for i in range(8):
        arrived(f"grad{i}")
    for r in range(D):
        top = gh[:, pl.ds(r * TC, TC)].astype(F32)
        place(g2, r, jnp.where(row > 0, top, 0.0))
        bottom = gh[:, pl.ds(OWN + TILE + r * TC, TC)].astype(F32)
        place(g2, D + TR + r, jnp.where(row < nr - 1, bottom, 0.0))
    clear_edges(kl, kr)
    set_edges(g2, kl, kr)
    arrived("rs")
    zb[zi] = jnp.sum(rs_recv[...].astype(F32), axis=0)

    def z_copy(k):
        return pltpu.make_async_remote_copy(
            zb.at[zi], zb.at[zi], red_sems.at[2], red_sems.at[3], z_peer(k), MESH
        )

    start_all(z_copy, nz)
    wait_later(zb.at[pl.ds(0, nz - 1)], red_sems.at[2], red_sems.at[3], "z")
    root = math.sqrt(bins)
    col_sum = jnp.zeros((C, TC), F32)
    row_sum = jnp.zeros((C, TC), F32)
    for i in range(TR // 2):
        here = pl.ds(OWN + i * 256, 256)
        act_grad = sum(
            dot(wd[p], g2[:, pl.ds(p * OWN + i * 256, 256)]) for p in range(3)
        )
        active = s2[pl.ds(C, C), here].astype(F32)
        pre_grad = jnp.where(active > 0, act_grad, 0.0)
        col_sum += pre_grad[:, :TC] + pre_grad[:, TC:]
        pair_grad = pre_grad + c2[:, here].astype(F32)
        for half in range(2):
            r = 2 * i + half
            part = slice(half * TC, half * TC + TC)
            row_sum = jnp.where(
                lane == r, jnp.sum(pre_grad[:, part], axis=1, keepdims=True), row_sum
            )
            xs[pl.ds(r, C, stride=TR), :] = pair_grad[:, part]
    cacc[...] = col_sum
    for i in range(nr):
        cgs[i] = cacc[pl.ds(i * cpr, cpr), :]
    rgs[...] = row_sum.reshape(nc, cpc, TC)

    def cg_copy(k):
        idx = lax.rem(row + k, nr)
        return pltpu.make_async_remote_copy(
            cgs.at[idx], cgr.at[row], out_sems.at[0], out_sems.at[1], row_peer(k), MESH
        )

    def rg_copy(k):
        idx = lax.rem(col + k, nc)
        return pltpu.make_async_remote_copy(
            rgs.at[idx], rgr.at[col], out_sems.at[2], out_sems.at[3], col_peer(k), MESH
        )

    start_all(cg_copy, nr)
    start_all(rg_copy, nc)
    wait_later(cgs.at[pl.ds(0, nr - 1)], out_sems.at[0], out_sems.at[1], "cg")
    wait_later(rgs.at[pl.ds(0, nc - 1)], out_sems.at[2], out_sems.at[3], "rg")
    cgr[row] = cgs[row]
    rgr[col] = rgs[col]

    arrived("z")
    ag[ai] = (jnp.sum(zb[...], axis=0) * (1.0 / bins)).astype(BF16)

    def ag_copy(k):
        return pltpu.make_async_remote_copy(
            ag.at[ai], ag.at[ai], red_sems.at[4], red_sems.at[5], a_peer(k), MESH
        )

    start_all(ag_copy, na)
    wait_later(ag.at[pl.ds(0, na - 1)], red_sems.at[4], red_sems.at[5], "ag")

    for i in range(8):
        pg_ref[pl.ds(i * 8, 8)] = xs[pl.ds(i * 256, 256), :].reshape(8, TR, TC).astype(BF16)

    arrived("cg")
    arrived("rg")
    colg_ref[...] = jnp.sum(cgr[...], axis=0) * (1.0 / root)
    rowg_ref[...] = jnp.sum(rgr[...], axis=0)[:, :TR] * (1.0 / root)

    store(0, 1)
    arrived("ag")
    store(1, 3)
    total = ag[...].astype(F32)
    low = total[:, :cr].reshape(256, TC)
    high = total[:, cr:].reshape(256, TC)
    for p in range(3):
        convg_ref[3 * p] = low[C * p : C * p + C, :C]
        convg_ref[3 * p + 1] = low[C * p : C * p + C, C:]
        convg_ref[3 * p + 2] = high[C * p : C * p + C, :C]
    projg_ref[...] = high[3 * C :, C:]
    gaing_ref[...] = jnp.sum(jnp.where(eye, high[:C, C : C + 1], 0.0), axis=0, keepdims=True)
    shiftg_ref[...] = jnp.sum(jnp.where(eye, high[:C, C + 1 : C + 2], 0.0), axis=0, keepdims=True)

    store(3, 7)
    for wait in (*recvs.values(), *pending):
        wait()


def store_kernel(*refs):
    sources, targets, stages, sems = refs[:7], refs[7:14], refs[14:21], refs[21]
    loads = [
        pltpu.make_async_copy(a, b, sems.at[i]) for i, (a, b) in enumerate(zip(sources, stages))
    ]
    stores = [
        pltpu.make_async_copy(a, b, sems.at[i]) for i, (a, b) in enumerate(zip(stages, targets))
    ]
    for copy in loads:
        copy.start()
    for load, store in zip(loads, stores):
        load.wait()
        store.start()
    for copy in stores:
        copy.wait()


def shards(nr, nc, pair_in, row_feat, col_feat, cotangent, conv_weight, gain, shift, proj):
    na, nz = 4 * nc, nr // 4
    cr = 256 // na
    hbm = pl.BlockSpec(memory_space=pltpu.HBM)
    scratch = dict(
        pg_ref=pltpu.VMEM((C, TR, TC), BF16),
        rowg_ref=pltpu.VMEM((C // nc, TR), F32),
        colg_ref=pltpu.VMEM((C // nr, TC), F32),
        convg_ref=pltpu.VMEM((9, C, C), F32),
        projg_ref=pltpu.VMEM((C, C), F32),
        gaing_ref=pltpu.VMEM((1, C), F32),
        shiftg_ref=pltpu.VMEM((1, C), F32),
        pair_ref=pltpu.VMEM((C, TR, TC), BF16),
        rowf_ref=pltpu.VMEM((C // nc, TR), BF16),
        colf_ref=pltpu.VMEM((C // nr, TC), BF16),
        cot_ref=pltpu.VMEM((C, TR, TC), BF16),
        w_ref=pltpu.VMEM((9, C, C), BF16),
        gain_ref=pltpu.VMEM((1, C), F32),
        shift_ref=pltpu.VMEM((1, C), F32),
        proj_ref=pltpu.VMEM((C, C), BF16),
        xs=pltpu.VMEM((C * TR, TC), F32),
        wf=pltpu.VMEM((3, C, 3 * C), BF16),
        pt=pltpu.VMEM((C, C), BF16),
        wd=pltpu.VMEM((3, C, 3 * C), BF16),
        gainb=pltpu.VMEM((C, 2 * TC), F32),
        shiftb=pltpu.VMEM((C, 2 * TC), F32),
        rf=pltpu.VMEM((nc, C // nc, TC), F32),
        cf=pltpu.VMEM((nr, C // nr, TC), F32),
        cfull=pltpu.VMEM((C, TC), F32),
        pc=pltpu.VMEM((C, LANES), BF16),
        rsend=pltpu.VMEM((C, TC), BF16),
        csend=pltpu.VMEM((C, TC), BF16),
        rnear=pltpu.VMEM((2, C, TC), BF16),
        cnear=pltpu.VMEM((2, C, TC), BF16),
        s2=pltpu.VMEM((4 * C, LANES), BF16),
        gh=pltpu.VMEM((C, LANES), BF16),
        c2=pltpu.VMEM((C, LANES), BF16),
        pkl=pltpu.VMEM((2, C, TC), BF16),
        pkr=pltpu.VMEM((2, C, TC), BF16),
        hl=pltpu.VMEM((4, C, TC), BF16),
        hr=pltpu.VMEM((4, C, TC), BF16),
        gz=pltpu.VMEM((C, LANES + 2 * OWN), BF16),
        g2=pltpu.VMEM((3 * C, LANES), BF16),
        qkl=pltpu.VMEM((2, C, TC), BF16),
        qkr=pltpu.VMEM((2, C, TC), BF16),
        kl=pltpu.VMEM((4, C, TC), BF16),
        kr=pltpu.VMEM((4, C, TC), BF16),
        wacc=pltpu.VMEM((4 * C, 4 * C), F32),
        rs_send=pltpu.VMEM((na, 2 * cr, TC), BF16),
        rs_recv=pltpu.VMEM((na, 2 * cr, TC), BF16),
        zb=pltpu.VMEM((nz, 2 * cr, TC), F32),
        ag=pltpu.VMEM((na, 2 * cr, TC), BF16),
        cacc=pltpu.VMEM((C, TC), F32),
        cgs=pltpu.VMEM((nr, C // nr, TC), F32),
        cgr=pltpu.VMEM((nr, C // nr, TC), F32),
        rgs=pltpu.VMEM((nc, C // nc, TC), F32),
        rgr=pltpu.VMEM((nc, C // nc, TC), F32),
        in_sems=pltpu.SemaphoreType.DMA((8,)),
        store_sems=pltpu.SemaphoreType.DMA((7,)),
        feat_sems=pltpu.SemaphoreType.DMA((4,)),
        side_sems=pltpu.SemaphoreType.DMA((8,)),
        halo_send=pltpu.SemaphoreType.DMA((8,)),
        halo_recv=pltpu.SemaphoreType.DMA((8,)),
        grad_send=pltpu.SemaphoreType.DMA((8,)),
        grad_recv=pltpu.SemaphoreType.DMA((8,)),
        red_sems=pltpu.SemaphoreType.DMA((6,)),
        out_sems=pltpu.SemaphoreType.DMA((4,)),
    )
    shapes = (
        jax.ShapeDtypeStruct((C, TR, TC), BF16),
        jax.ShapeDtypeStruct((C // nc, TR), F32),
        jax.ShapeDtypeStruct((C // nr, TC), F32),
        jax.ShapeDtypeStruct((9, C, C), F32),
        jax.ShapeDtypeStruct((C, C), F32),
        jax.ShapeDtypeStruct((1, C), F32),
        jax.ShapeDtypeStruct((1, C), F32),
    )
    outs = pl.pallas_call(
        functools.partial(kernel, nr, nc),
        out_shape=shapes,
        in_specs=[hbm] * 8,
        out_specs=(hbm,) * 7,
        scratch_shapes=list(scratch.values()),
        compiler_params=pltpu.CompilerParams(
            collective_id=0, has_side_effects=True, vmem_limit_bytes=VMEM_LIMIT
        ),
    )(
        pair_in,
        row_feat,
        col_feat,
        cotangent,
        conv_weight,
        gain.reshape(1, C),
        shift.reshape(1, C),
        proj,
    )
    outs = pl.pallas_call(
        store_kernel,
        out_shape=shapes,
        in_specs=[hbm] * 7,
        out_specs=(hbm,) * 7,
        scratch_shapes=[
            *(pltpu.VMEM(shape.shape, shape.dtype) for shape in shapes),
            pltpu.SemaphoreType.DMA((7,)),
        ],
        compiler_params=pltpu.CompilerParams(vmem_limit_bytes=VMEM_LIMIT),
    )(*outs)
    return (*outs[:5], outs[5].reshape(C), outs[6].reshape(C))


def solution(mesh):
    return jax.shard_map(
        functools.partial(shards, mesh.shape["row"], mesh.shape["col"]),
        mesh=mesh,
        in_specs=(
            P(None, "row", "col"),
            P("col", "row"),
            P("row", "col"),
            P(None, "row", "col"),
            P(),
            P(),
            P(),
            P(),
        ),
        out_specs=(P(None, "row", "col"), P("col", "row"), P("row", "col"), P(), P(), P(), P()),
        check_vma=False,
    )
```

time: 65.6 us -> 47.6 us (0.73)
  Pallas kernels: 56 us -> 46.8 us
  local copies, waits for them, and re-layouts: 8.68 us -> 0 us
    pallas_call x1 -> x2, Pallas kernels: 56 us -> 46.8 us  [the longest x1 44.8 us: shards(): pl.pallas_call(functools.partial(kernel, nr, nc), out_shape=shapes, in_sp...]
    unnamed x23 -> x0, local copies, waits for them, and re-layouts: 8.68 us -> none
where the time goes in v2:
time: 47.6 us; the launch traced here: 47.5 us
  Pallas kernels  46.8 us (98%)
  between operations  0.64 us (1%)
    pallas_call x1, Pallas kernels, shards(): pl.pallas_call(functools.partial(kernel, nr, nc), out_shape=shapes, in_sp...  44.8 us
    pallas_call x1, Pallas kernels, shards(): pl.pallas_call(store_kernel, out_shape=shapes, in_specs=[hbm] * 7, out_sp...  2 us

profile of v2, /device:TPU:1, one launch (start us, length us, event | category | flops | bytes accessed | tf_op | source)
XLA Modules:
  0.0 47.5 jit_solution(3933094075298372531)
XLA Ops:
  0.6 44.8 %shard_map.135 = (bf16[64,32,128]{2,1,0:T(8,128)(2,1)}, f32[8,32]{1,0:T(8,128)}, f32[2,128]{1,0:T(2,128)}, f32[9,64,64]{2,1,0:T(8,128)}, f32[64,64]{1,0:T(8,128)}, /*index=5*/f32[1,64]{1,0:T(1,128)}, f32[1,64]{1,0:T(1,128)}) custom-call(bf16[64,32,128]{2,1,0:T(8,128)(2,1)} %pair_in.1, bf16[8,32]{1,0:T(8,128)(2,1)} %rowf_in.1, bf16[2,128]{1,0:T(2,128)(2,1)} %colf_in.1, ...), custom_call_target="tpu_custom_call" | custom-call | tf_op jit(solution)/shard_map/pallas_call | solution.py:668
  45.5 2.0 %shard_map.136 = (bf16[64,32,128]{2,1,0:T(8,128)(2,1)}, f32[8,32]{1,0:T(8,128)}, f32[2,128]{1,0:T(2,128)}, f32[9,64,64]{2,1,0:T(8,128)}, f32[64,64]{1,0:T(8,128)}, /*index=5*/f32[1,64]{1,0:T(1,128)}, f32[1,64]{1,0:T(1,128)}) custom-call(bf16[64,32,128]{2,1,0:T(8,128)(2,1)} %get-tuple-element.21.refs_0_, f32[8,32]{1,0:T(8,128)} %get-tuple-element.22.refs_1_, ...), custom_call_target="tpu_custom_call" | custom-call | tf_op jit(solution)/shard_map/pallas_call | solution.py:687

commit v3 on v2

--- a/solution.py
+++ b/solution.py
@@ -18,7 +18,7 @@
 TILE = TR * TC
 F32 = jnp.float32
 BF16 = jnp.bfloat16
-VMEM_LIMIT = 60 * 1024 * 1024
+VMEM_LIMIT = 40 * 1024 * 1024
 MESH = pl.DeviceIdType.MESH
 
 
@@ -41,13 +41,6 @@
     gain_in,
     shift_in,
     proj_in,
-    pg_out,
-    rowg_out,
-    colg_out,
-    convg_out,
-    projg_out,
-    gaing_out,
-    shiftg_out,
     pg_ref,
     rowg_ref,
     colg_ref,
@@ -101,7 +94,6 @@
     rgs,
     rgr,
     in_sems,
-    store_sems,
     feat_sems,
     side_sems,
     halo_send,
@@ -137,17 +129,17 @@
     def z_peer(k):
         return (lax.rem(zi + k, nz) * 4 + lax.rem(row, 4), col)
 
+    def far_first(count, ring):
+        return sorted(range(1, count), key=lambda k: -min(k % ring, ring - k % ring))
+
     barrier = pltpu.get_barrier_semaphore()
 
-    def greet(peer, count):
-        def body(k, _):
+    def greet(peer, count, ring):
+        for k in far_first(count, ring):
             pl.semaphore_signal(barrier, inc=1, device_id=peer(k), device_id_type=MESH)
-            return 0
-
-        lax.fori_loop(1, count, body, 0)
-
-    greet(row_peer, nr)
-    greet(a_peer, na)
+
+    greet(row_peer, nr, nr)
+    greet(a_peer, na, nc)
     for dr in (up, down):
         for dc in (left, right):
             pl.semaphore_signal(barrier, inc=1, device_id=(dr, dc), device_id_type=MESH)
@@ -171,32 +163,15 @@
         load.start()
     pending = []
     recvs = {}
-    outputs = (
-        (pg_ref, pg_out),
-        (rowg_ref, rowg_out),
-        (colg_ref, colg_out),
-        (convg_ref, convg_out),
-        (projg_ref, projg_out),
-        (gaing_ref, gaing_out),
-        (shiftg_ref, shiftg_out),
-    )
-
-    def store(first, last):
-        for i in range(first, last):
-            copy = pltpu.make_async_copy(*outputs[i], store_sems.at[i])
-            copy.start()
-            pending.append(copy.wait)
-
-
     lane = lax.broadcasted_iota(jnp.int32, (C, TC), 1)
 
     def packed(parts, edge):
-        result = jnp.zeros((C, TC), F32)
+        result = jnp.zeros((C, TC), BF16)
         for k, x in enumerate(parts):
             shift = (8 * k + edge) % TC
             moved = pltpu.roll(x, shift, 1) if shift else x
             result = jnp.where(lane // 8 == k, moved, result)
-        return result.astype(BF16)
+        return result
 
     def halo_copies(center, base, target, lsend, rsend, lrecv, rrecv, ssem, rsem):
         plan = (
@@ -243,8 +218,7 @@
 
     def set_edges(ref, lrecv, rrecv):
         for b in range(4):
-            lo = lrecv[b].astype(F32)
-            hi = rrecv[b].astype(F32)
+            lo, hi = lrecv[b], rrecv[b]
             for k in range(16):
                 r = 16 * b + k - 8
                 if not 0 <= r < PR:
@@ -253,12 +227,8 @@
                 from_right = pltpu.roll(hi, 120 - 8 * k, 1) if k < 15 else hi
                 at_left = ref.at[pl.ds(0, C), pl.ds(r * TC, TC)]
                 at_right = ref.at[pl.ds(2 * C, C), pl.ds(r * TC, TC)]
-                at_left[...] = jnp.where(
-                    lane < 8, from_left, at_left[...].astype(F32)
-                ).astype(BF16)
-                at_right[...] = jnp.where(
-                    lane >= 120, from_right, at_right[...].astype(F32)
-                ).astype(BF16)
+                at_left[...] = jnp.where(lane < 8, from_left, at_left[...])
+                at_right[...] = jnp.where(lane >= 120, from_right, at_right[...])
 
     for i in range(3):
         loads[i].wait()
@@ -272,8 +242,8 @@
         parts = []
         for k in range(16):
             r = 16 * b + k
-            x = xs[pl.ds(r, C, stride=TR), :]
-            pc[:, pl.ds(OWN + r * TC, TC)] = x.astype(BF16)
+            x = xs[pl.ds(r, C, stride=TR), :].astype(BF16)
+            pc[:, pl.ds(OWN + r * TC, TC)] = x
             parts.append(x)
         pkl[b] = packed(parts, 0)
         pkr[b] = packed(parts, 8)
@@ -290,12 +260,9 @@
             cf.at[row], cf.at[row], feat_sems.at[2], feat_sems.at[3], row_peer(k), MESH
         )
 
-    def start_all(copy, count):
-        def body(k, _):
+    def start_all(copy, count, ring):
+        for k in far_first(count, ring):
             copy(k).start()
-            return 0
-
-        lax.fori_loop(1, count, body, 0)
 
     def wait_bytes(ref, sem):
         pltpu.make_async_copy(ref, ref, sem).wait()
@@ -307,8 +274,8 @@
     def arrived(name):
         recvs.pop(name)()
 
-    start_all(rf_copy, nc)
-    start_all(cf_copy, nr)
+    start_all(cf_copy, nr, nr)
+    start_all(rf_copy, nc, nc)
     wait_later(rf.at[pl.ds(0, nc - 1)], feat_sems.at[0], feat_sems.at[1], "rf")
     wait_later(cf.at[pl.ds(0, nr - 1)], feat_sems.at[2], feat_sems.at[3], "cf")
     copies = halo_copies(pc, OWN, pc, pkl, pkr, hl, hr, halo_send, halo_recv)
@@ -368,12 +335,12 @@
 
     def activate(r, rows, at):
         pre = pc[:, pl.ds(r * TC, TC)].astype(F32) + rows[:, at : at + 1] + col_full
-        return jnp.maximum(pre, 0.0)
+        return jnp.maximum(pre, 0.0).astype(BF16)
 
     def place(ref, r, x):
-        ref[pl.ds(0, C), pl.ds(r * TC, TC)] = pltpu.roll(x, 8, 1).astype(BF16)
-        ref[pl.ds(C, C), pl.ds(r * TC, TC)] = x.astype(BF16)
-        ref[pl.ds(2 * C, C), pl.ds(r * TC, TC)] = pltpu.roll(x, 120, 1).astype(BF16)
+        ref[pl.ds(0, C), pl.ds(r * TC, TC)] = pltpu.roll(x, 8, 1)
+        ref[pl.ds(C, C), pl.ds(r * TC, TC)] = x
+        ref[pl.ds(2 * C, C), pl.ds(r * TC, TC)] = pltpu.roll(x, 120, 1)
 
     for r in range(TR):
         place(s2, D + r, activate(D + r, row_full, r))
@@ -384,9 +351,9 @@
     above, below = rnear[0].astype(F32), rnear[1].astype(F32)
     for r in range(D):
         top = activate(r, above, TR - D + r)
-        place(s2, r, jnp.where(row > 0, top, 0.0))
+        place(s2, r, jnp.where(row > 0, top, jnp.zeros_like(top)))
         bottom = activate(D + TR + r, below, r)
-        place(s2, D + TR + r, jnp.where(row < nr - 1, bottom, 0.0))
+        place(s2, D + TR + r, jnp.where(row < nr - 1, bottom, jnp.zeros_like(bottom)))
 
     def spread(first, divide):
         source = lax.broadcasted_iota(jnp.int32, (TC, TC), 0)
@@ -427,16 +394,10 @@
         gz[:, pl.ds(2 * OWN + i * 256, 256)] = (gain * normed_grad).astype(BF16)
     for b in range(2):
         parts = [
-            gz[:, pl.ds(2 * OWN + (16 * b + k) * TC, TC)].astype(F32) for k in range(16)
+            gz[:, pl.ds(2 * OWN + (16 * b + k) * TC, TC)] for k in range(16)
         ]
         qkl[b] = packed(parts, 0)
         qkr[b] = packed(parts, 8)
-    grad_copies = halo_copies(gz, 2 * OWN, gh, qkl, qkr, kl, kr, grad_send, grad_recv)
-    for i, copy in enumerate(grad_copies):
-        copy.start()
-        pending.append(copy.wait_send)
-        recvs[f"grad{i}"] = copy.wait_recv
-
     total = jnp.zeros((4 * C, 4 * C), F32)
     step = 1024
     for base in range(0, LANES, step):
@@ -465,31 +426,37 @@
             rs_send.at[idx], rs_recv.at[ai], red_sems.at[0], red_sems.at[1], a_peer(k), MESH
         )
 
-    start_all(rs_copy, na)
+    start_all(rs_copy, na, nc)
     wait_later(rs_send.at[pl.ds(0, na - 1)], red_sems.at[0], red_sems.at[1], "rs")
     rs_recv[ai] = rs_send[ai]
 
+    grad_copies = halo_copies(gz, 2 * OWN, gh, qkl, qkr, kl, kr, grad_send, grad_recv)
+    for i, copy in enumerate(grad_copies):
+        copy.start()
+        pending.append(copy.wait_send)
+        recvs[f"grad{i}"] = copy.wait_recv
+
     for r in range(TR):
-        place(g2, D + r, gz[:, pl.ds(2 * OWN + r * TC, TC)].astype(F32))
+        place(g2, D + r, gz[:, pl.ds(2 * OWN + r * TC, TC)])
+    arrived("rs")
+    zb[zi] = jnp.sum(rs_recv[...].astype(F32), axis=0)
+
+    def z_copy(k):
+        return pltpu.make_async_remote_copy(
+            zb.at[zi], zb.at[zi], red_sems.at[2], red_sems.at[3], z_peer(k), MESH
+        )
+
+    start_all(z_copy, nz, nz)
+    wait_later(zb.at[pl.ds(0, nz - 1)], red_sems.at[2], red_sems.at[3], "z")
     for i in range(8):
         arrived(f"grad{i}")
     for r in range(D):
-        top = gh[:, pl.ds(r * TC, TC)].astype(F32)
-        place(g2, r, jnp.where(row > 0, top, 0.0))
-        bottom = gh[:, pl.ds(OWN + TILE + r * TC, TC)].astype(F32)
-        place(g2, D + TR + r, jnp.where(row < nr - 1, bottom, 0.0))
+        top = gh[:, pl.ds(r * TC, TC)]
+        place(g2, r, jnp.where(row > 0, top, jnp.zeros_like(top)))
+        bottom = gh[:, pl.ds(OWN + TILE + r * TC, TC)]
+        place(g2, D + TR + r, jnp.where(row < nr - 1, bottom, jnp.zeros_like(bottom)))
     clear_edges(kl, kr)
     set_edges(g2, kl, kr)
-    arrived("rs")
-    zb[zi] = jnp.sum(rs_recv[...].astype(F32), axis=0)
-
-    def z_copy(k):
-        return pltpu.make_async_remote_copy(
-            zb.at[zi], zb.at[zi], red_sems.at[2], red_sems.at[3], z_peer(k), MESH
-        )
-
-    start_all(z_copy, nz)
-    wait_later(zb.at[pl.ds(0, nz - 1)], red_sems.at[2], red_sems.at[3], "z")
     root = math.sqrt(bins)
     col_sum = jnp.zeros((C, TC), F32)
     row_sum = jnp.zeros((C, TC), F32)
@@ -526,8 +493,8 @@
             rgs.at[idx], rgr.at[col], out_sems.at[2], out_sems.at[3], col_peer(k), MESH
         )
 
-    start_all(cg_copy, nr)
-    start_all(rg_copy, nc)
+    start_all(cg_copy, nr, nr)
+    start_all(rg_copy, nc, nc)
     wait_later(cgs.at[pl.ds(0, nr - 1)], out_sems.at[0], out_sems.at[1], "cg")
     wait_later(rgs.at[pl.ds(0, nc - 1)], out_sems.at[2], out_sems.at[3], "rg")
     cgr[row] = cgs[row]
@@ -541,7 +508,7 @@
             ag.at[ai], ag.at[ai], red_sems.at[4], red_sems.at[5], a_peer(k), MESH
         )
 
-    start_all(ag_copy, na)
+    start_all(ag_copy, na, nc)
     wait_later(ag.at[pl.ds(0, na - 1)], red_sems.at[4], red_sems.at[5], "ag")
 
     for i in range(8):
@@ -552,9 +519,7 @@
     colg_ref[...] = jnp.sum(cgr[...], axis=0) * (1.0 / root)
     rowg_ref[...] = jnp.sum(rgr[...], axis=0)[:, :TR] * (1.0 / root)
 
-    store(0, 1)
     arrived("ag")
-    store(1, 3)
     total = ag[...].astype(F32)
     low = total[:, :cr].reshape(256, TC)
     high = total[:, cr:].reshape(256, TC)
@@ -566,25 +531,17 @@
     gaing_ref[...] = jnp.sum(jnp.where(eye, high[:C, C : C + 1], 0.0), axis=0, keepdims=True)
     shiftg_ref[...] = jnp.sum(jnp.where(eye, high[:C, C + 1 : C + 2], 0.0), axis=0, keepdims=True)
 
-    store(3, 7)
     for wait in (*recvs.values(), *pending):
         wait()
 
 
 def store_kernel(*refs):
-    sources, targets, stages, sems = refs[:7], refs[7:14], refs[14:21], refs[21]
-    loads = [
-        pltpu.make_async_copy(a, b, sems.at[i]) for i, (a, b) in enumerate(zip(sources, stages))
+    copies = [
+        pltpu.make_async_copy(refs[i], refs[7 + i], refs[14].at[i]) for i in range(7)
     ]
-    stores = [
-        pltpu.make_async_copy(a, b, sems.at[i]) for i, (a, b) in enumerate(zip(stages, targets))
-    ]
-    for copy in loads:
+    for copy in copies:
         copy.start()
-    for load, store in zip(loads, stores):
-        load.wait()
-        store.start()
-    for copy in stores:
+    for copy in copies:
         copy.wait()
 
 
@@ -592,14 +549,8 @@
     na, nz = 4 * nc, nr // 4
     cr = 256 // na
     hbm = pl.BlockSpec(memory_space=pltpu.HBM)
+    vmem = pl.BlockSpec(memory_space=pltpu.VMEM)
     scratch = dict(
-        pg_ref=pltpu.VMEM((C, TR, TC), BF16),
-        rowg_ref=pltpu.VMEM((C // nc, TR), F32),
-        colg_ref=pltpu.VMEM((C // nr, TC), F32),
-        convg_ref=pltpu.VMEM((9, C, C), F32),
-        projg_ref=pltpu.VMEM((C, C), F32),
-        gaing_ref=pltpu.VMEM((1, C), F32),
-        shiftg_ref=pltpu.VMEM((1, C), F32),
         pair_ref=pltpu.VMEM((C, TR, TC), BF16),
         rowf_ref=pltpu.VMEM((C // nc, TR), BF16),
         colf_ref=pltpu.VMEM((C // nr, TC), BF16),
@@ -646,7 +597,6 @@
         rgs=pltpu.VMEM((nc, C // nc, TC), F32),
         rgr=pltpu.VMEM((nc, C // nc, TC), F32),
         in_sems=pltpu.SemaphoreType.DMA((8,)),
-        store_sems=pltpu.SemaphoreType.DMA((7,)),
         feat_sems=pltpu.SemaphoreType.DMA((4,)),
         side_sems=pltpu.SemaphoreType.DMA((8,)),
         halo_send=pltpu.SemaphoreType.DMA((8,)),
@@ -667,33 +617,35 @@
     )
     outs = pl.pallas_call(
         functools.partial(kernel, nr, nc),
-        out_shape=shapes,
+        out_shape=tuple(pltpu.VMEM(shape.shape, shape.dtype) for shape in shapes),
         in_specs=[hbm] * 8,
-        out_specs=(hbm,) * 7,
+        out_specs=(vmem,) * 7,
         scratch_shapes=list(scratch.values()),
         compiler_params=pltpu.CompilerParams(
             collective_id=0, has_side_effects=True, vmem_limit_bytes=VMEM_LIMIT
         ),
     )(
-        pair_in,
-        row_feat,
-        col_feat,
-        cotangent,
-        conv_weight,
-        gain.reshape(1, C),
-        shift.reshape(1, C),
-        proj,
+        *(
+            pltpu.with_memory_space_constraint(operand, pltpu.HBM)
+            for operand in (
+                pair_in,
+                row_feat,
+                col_feat,
+                cotangent,
+                conv_weight,
+                gain.reshape(1, C),
+                shift.reshape(1, C),
+                proj,
+            )
+        )
     )
     outs = pl.pallas_call(
         store_kernel,
         out_shape=shapes,
-        in_specs=[hbm] * 7,
+        in_specs=[vmem] * 7,
         out_specs=(hbm,) * 7,
-        scratch_shapes=[
-            *(pltpu.VMEM(shape.shape, shape.dtype) for shape in shapes),
-            pltpu.SemaphoreType.DMA((7,)),
-        ],
-        compiler_params=pltpu.CompilerParams(vmem_limit_bytes=VMEM_LIMIT),
+        scratch_shapes=[pltpu.SemaphoreType.DMA((7,))],
+        compiler_params=pltpu.CompilerParams(vmem_limit_bytes=8 * 1024 * 1024),
     )(*outs)
     return (*outs[:5], outs[5].reshape(C), outs[6].reshape(C))
 

time: 47.6 us -> 44.3 us (0.931)
  Pallas kernels: 46.8 us -> 43.5 us
    pallas_call x2, Pallas kernels: 46.8 us -> 43.5 us  [the longest x1 42.5 us: shards(): pl.pallas_call(functools.partial(kernel, nr, nc), out_shape=tuple((pltpu....]
where the time goes in v3:
time: 44.3 us; the launch traced here: 44.2 us
  Pallas kernels  43.5 us (98%)
  between operations  0.64 us (1%)
    pallas_call x1, Pallas kernels, shards(): pl.pallas_call(functools.partial(kernel, nr, nc), out_shape=tuple((pltpu....  42.5 us
    pallas_call x1, Pallas kernels, shards(): pl.pallas_call(store_kernel, out_shape=shapes, in_specs=[vmem] * 7, out_s...  0.97 us

profile of v3, /device:TPU:1, one launch (start us, length us, event | category | flops | bytes accessed | tf_op | source)
XLA Modules:
  0.0 44.2 jit_solution(8109043261091185197)
XLA Ops:
  0.6 42.5 %shard_map.135 = (bf16[64,32,128]{2,1,0:T(8,128)(2,1)S(1)}, f32[8,32]{1,0:T(8,128)S(1)}, f32[2,128]{1,0:T(2,128)S(1)}, f32[9,64,64]{2,1,0:T(8,128)S(1)}, f32[64,...) custom-call(bf16[64,32,128]{2,1,0:T(8,128)(2,1)} %pair_in.1, bf16[8,32]{1,0:T(8,128)(2,1)} %rowf_in.1, ...), custom_call_target="tpu_custom_call" | custom-call | tf_op jit(solution)/shard_map/pallas_call | solution.py:618
  43.2 1.0 %shard_map.136 = (bf16[64,32,128]{2,1,0:T(8,128)(2,1)}, f32[8,32]{1,0:T(8,128)}, f32[2,128]{1,0:T(2,128)}, f32[9,64,64]{2,1,0:T(8,128)}, f32[64,64]{1,0:T(8,128)}, /*index=5*/f32[1,64]{1,0:T(1,128)}, f32[1,64]{1,0:T(1,128)}) custom-call(bf16[64,32,128]{2,1,0:T(8,128)(2,1)S(1)} %get-tuple-element.21.refs_0_, f32[8,32]{1,0:T(8,128)S(1)} %get-tuple-element.22.refs_1_, ...), custom_call_target="tpu_custom_call" | custom-call | tf_op jit(solution)/shard_map/pallas_call | solution.py:642

commit v4 on v3

--- a/solution.py
+++ b/solution.py
@@ -138,12 +138,11 @@
         for k in far_first(count, ring):
             pl.semaphore_signal(barrier, inc=1, device_id=peer(k), device_id_type=MESH)
 
-    greet(row_peer, nr, nr)
-    greet(a_peer, na, nc)
     for dr in (up, down):
         for dc in (left, right):
             pl.semaphore_signal(barrier, inc=1, device_id=(dr, dc), device_id_type=MESH)
-
+    greet(row_peer, nr, nr)
+    greet(a_peer, na, nc)
     loads = [
         pltpu.make_async_copy(src, dst, in_sems.at[i])
         for i, (src, dst) in enumerate(
@@ -378,7 +377,17 @@
     gain, shift = gainb[...], shiftb[...]
     gain_sum = jnp.zeros((C, TC), F32)
     shift_sum = jnp.zeros((C, TC), F32)
-    for i in range(TR // 2):
+    grad_copies = halo_copies(gz, 2 * OWN, gh, qkl, qkr, kl, kr, grad_send, grad_recv)
+
+    def send_grads(which):
+        for i in which:
+            grad_copies[i].start()
+            pending.append(grad_copies[i].wait_send)
+            recvs[f"grad{i}"] = grad_copies[i].wait_recv
+
+    for i in (0, 1, 2, 3, 12, 13, 14, 15, 4, 5, 6, 7, 8, 9, 10, 11):
+        if i == 4:
+            send_grads((6, 7))
         here = pl.ds(OWN + i * 256, 256)
         conv_out = sum(
             dot(wf[p], s2[pl.ds(0, 3 * C), pl.ds(p * OWN + i * 256, 256)]) for p in range(3)
@@ -430,16 +439,12 @@
     wait_later(rs_send.at[pl.ds(0, na - 1)], red_sems.at[0], red_sems.at[1], "rs")
     rs_recv[ai] = rs_send[ai]
 
-    grad_copies = halo_copies(gz, 2 * OWN, gh, qkl, qkr, kl, kr, grad_send, grad_recv)
-    for i, copy in enumerate(grad_copies):
-        copy.start()
-        pending.append(copy.wait_send)
-        recvs[f"grad{i}"] = copy.wait_recv
+    send_grads(range(6))
 
     for r in range(TR):
         place(g2, D + r, gz[:, pl.ds(2 * OWN + r * TC, TC)])
     arrived("rs")
-    zb[zi] = jnp.sum(rs_recv[...].astype(F32), axis=0)
+    zb[zi] = jnp.sum(rs_recv[...].astype(F32), axis=0).astype(BF16)
 
     def z_copy(k):
         return pltpu.make_async_remote_copy(
@@ -501,7 +506,7 @@
     rgr[col] = rgs[col]
 
     arrived("z")
-    ag[ai] = (jnp.sum(zb[...], axis=0) * (1.0 / bins)).astype(BF16)
+    ag[ai] = (jnp.sum(zb[...].astype(F32), axis=0) * (1.0 / bins)).astype(BF16)
 
     def ag_copy(k):
         return pltpu.make_async_remote_copy(
@@ -589,7 +594,7 @@
         wacc=pltpu.VMEM((4 * C, 4 * C), F32),
         rs_send=pltpu.VMEM((na, 2 * cr, TC), BF16),
         rs_recv=pltpu.VMEM((na, 2 * cr, TC), BF16),
-        zb=pltpu.VMEM((nz, 2 * cr, TC), F32),
+        zb=pltpu.VMEM((nz, 2 * cr, TC), BF16),
         ag=pltpu.VMEM((na, 2 * cr, TC), BF16),
         cacc=pltpu.VMEM((C, TC), F32),
         cgs=pltpu.VMEM((nr, C // nr, TC), F32),

time: 44.3 us -> 43.5 us (0.982)
  Pallas kernels: 43.5 us -> 42.7 us
    pallas_call x1, Pallas kernels: 42.5 us -> 41.8 us  [shards(): pl.pallas_call(functools.partial(kernel, nr, nc), out_shape=tuple((pltpu....]
where the time goes in v4:
time: 43.5 us; the launch traced here: 43.4 us
  Pallas kernels  42.7 us (98%)
  between operations  0.64 us (1%)
    pallas_call x1, Pallas kernels, shards(): pl.pallas_call(functools.partial(kernel, nr, nc), out_shape=tuple((pltpu....  41.8 us
    pallas_call x1, Pallas kernels, shards(): pl.pallas_call(store_kernel, out_shape=shapes, in_specs=[vmem] * 7, out_s...  0.97 us

profile of v4, /device:TPU:1, one launch (start us, length us, event | category | flops | bytes accessed | tf_op | source)
XLA Modules:
  0.0 43.4 jit_solution(13312403598781734616)
XLA Ops:
  0.6 41.8 %shard_map.135 = (bf16[64,32,128]{2,1,0:T(8,128)(2,1)S(1)}, f32[8,32]{1,0:T(8,128)S(1)}, f32[2,128]{1,0:T(2,128)S(1)}, f32[9,64,64]{2,1,0:T(8,128)S(1)}, f32[64,...) custom-call(bf16[64,32,128]{2,1,0:T(8,128)(2,1)} %pair_in.1, bf16[8,32]{1,0:T(8,128)(2,1)} %rowf_in.1, ...), custom_call_target="tpu_custom_call" | custom-call | tf_op jit(solution)/shard_map/pallas_call | solution.py:623
  42.4 1.0 %shard_map.136 = (bf16[64,32,128]{2,1,0:T(8,128)(2,1)}, f32[8,32]{1,0:T(8,128)}, f32[2,128]{1,0:T(2,128)}, f32[9,64,64]{2,1,0:T(8,128)}, f32[64,64]{1,0:T(8,128)}, /*index=5*/f32[1,64]{1,0:T(1,128)}, f32[1,64]{1,0:T(1,128)}) custom-call(bf16[64,32,128]{2,1,0:T(8,128)(2,1)S(1)} %get-tuple-element.21.refs_0_, f32[8,32]{1,0:T(8,128)S(1)} %get-tuple-element.22.refs_1_, ...), custom_call_target="tpu_custom_call" | custom-call | tf_op jit(solution)/shard_map/pallas_call | solution.py:647

commit v5 on v4

--- a/solution.py
+++ b/solution.py
@@ -28,6 +28,11 @@
 
 def dot_nt(a, b):
     return lax.dot_general(a, b, (((1,), (1,)), ((), ())), preferred_element_type=F32)
+
+
+def chunking(na):
+    height = 16 * (32 // na)
+    return height, -(-(5 * C + 1) // height)
 
 
 def kernel(
@@ -107,11 +112,13 @@
     col = lax.axis_index("col")
     nz = nr // 4
     na = 4 * nc
-    cr = 256 // na
     cpr = C // nr
     cpc = C // nc
     zi = row // 4
     ai = lax.rem(row, 4) * nc + col
+    height, owners = chunking(na)
+    chunk = (ai * owners + na - 1) // na
+    owner = jnp.logical_and(chunk < owners, chunk * na // owners == ai)
     up, down = lax.rem(row + nr - 1, nr), lax.rem(row + 1, nr)
     left, right = lax.rem(col + nc - 1, nc), lax.rem(col + 1, nc)
     bins = TR * nr
@@ -385,9 +392,26 @@
             pending.append(grad_copies[i].wait_send)
             recvs[f"grad{i}"] = grad_copies[i].wait_recv
 
+    def weights(part):
+        base = part * OWN
+        lhs = jnp.concatenate(
+            [
+                gz[:, pl.ds(base + 2 * OWN, OWN)],
+                gz[:, pl.ds(base + OWN, OWN)],
+                gz[:, pl.ds(base, OWN)],
+                c2[:, pl.ds(base, OWN)],
+            ],
+            axis=0,
+        )
+        return dot_nt(lhs, s2[:, pl.ds(base, OWN)])
+
+    sums = []
     for i in (0, 1, 2, 3, 12, 13, 14, 15, 4, 5, 6, 7, 8, 9, 10, 11):
         if i == 4:
             send_grads((6, 7))
+            sums = [weights(0) + weights(5)]
+        if i == 8:
+            sums = [sums[0] + weights(1)]
         here = pl.ds(OWN + i * 256, 256)
         conv_out = sum(
             dot(wf[p], s2[pl.ds(0, 3 * C), pl.ds(p * OWN + i * 256, 256)]) for p in range(3)
@@ -407,52 +431,78 @@
         ]
         qkl[b] = packed(parts, 0)
         qkr[b] = packed(parts, 8)
-    total = jnp.zeros((4 * C, 4 * C), F32)
-    step = 1024
-    for base in range(0, LANES, step):
-        lhs = jnp.concatenate(
-            [
-                gz[:, pl.ds(base + 2 * OWN, step)],
-                gz[:, pl.ds(base + OWN, step)],
-                gz[:, pl.ds(base, step)],
-                c2[:, pl.ds(base, step)],
-            ],
-            axis=0,
-        )
-        total += dot_nt(lhs, s2[:, pl.ds(base, step)])
-    wacc[...] = total
-    wacc[pl.ds(0, C), pl.ds(3 * C, 1)] = jnp.sum(gain_sum, axis=1, keepdims=True)
-    wacc[pl.ds(0, C), pl.ds(3 * C + 1, 1)] = jnp.sum(shift_sum, axis=1, keepdims=True)
-
-    for a in range(na):
-        rs_send[a] = jnp.concatenate(
-            [wacc[pl.ds(a * cr, cr), pl.ds(0, TC)], wacc[pl.ds(a * cr, cr), pl.ds(TC, TC)]], axis=0
-        ).astype(BF16)
+    wacc[...] = sums[0] + weights(2) + weights(3) + weights(4)
+    sides = [
+        jnp.sum(jnp.where(eye, jnp.sum(part, axis=1, keepdims=True), 0.0), axis=0, keepdims=True)
+        for part in (gain_sum, shift_sum)
+    ]
+    low, high = wacc[:, :TC], wacc[:, TC:]
+    left_half = lane[:32] < C
+    pieces = [low[i * 32 : i * 32 + 32] for i in range(6)]
+    for i in range(3):
+        first, second = high[i * 32 : i * 32 + 32], high[96 + i * 32 : 128 + i * 32]
+        pieces.append(jnp.where(left_half, first, pltpu.roll(second, C, 1)))
+    pieces.append(jnp.where(left_half, pltpu.roll(high[192:224], C, 1), high[224:256]))
+    pieces.append(
+        jnp.broadcast_to(jnp.concatenate(sides, axis=1), (height * owners - 5 * C, TC))
+    )
+    packed_sums = jnp.concatenate(pieces, axis=0).astype(BF16)
+    for i in range(owners):
+        rs_send[i] = packed_sums[i * height : i * height + height]
+
+    def a_device(idx):
+        return (zi * 4 + idx // nc, lax.rem(idx, nc))
 
     def rs_copy(k):
-        idx = lax.rem(ai + k, na)
+        part = lax.rem(chunk + k, owners)
         return pltpu.make_async_remote_copy(
-            rs_send.at[idx], rs_recv.at[ai], red_sems.at[0], red_sems.at[1], a_peer(k), MESH
-        )
-
-    start_all(rs_copy, na, nc)
-    wait_later(rs_send.at[pl.ds(0, na - 1)], red_sems.at[0], red_sems.at[1], "rs")
-    rs_recv[ai] = rs_send[ai]
+            rs_send.at[part],
+            rs_recv.at[ai],
+            red_sems.at[0],
+            red_sems.at[1],
+            a_device(part * na // owners),
+            MESH,
+        )
+
+    start_all(rs_copy, owners, owners)
+
+    @pl.when(jnp.logical_not(owner))
+    def _():
+        rs_copy(0).start()
+
+    @pl.when(owner)
+    def _():
+        rs_recv[ai] = rs_send[chunk]
+
+    def wait_if_owner(ref, sem, when_owner, otherwise):
+        @pl.when(owner)
+        def _():
+            wait_bytes(ref.at[pl.ds(0, when_owner)], sem)
+
+        if otherwise:
+            @pl.when(jnp.logical_not(owner))
+            def _():
+                wait_bytes(ref.at[pl.ds(0, otherwise)], sem)
+
+    pending.append(lambda: wait_if_owner(rs_send, red_sems.at[0], owners - 1, owners))
 
     send_grads(range(6))
 
     for r in range(TR):
         place(g2, D + r, gz[:, pl.ds(2 * OWN + r * TC, TC)])
-    arrived("rs")
-    zb[zi] = jnp.sum(rs_recv[...].astype(F32), axis=0).astype(BF16)
-
     def z_copy(k):
         return pltpu.make_async_remote_copy(
             zb.at[zi], zb.at[zi], red_sems.at[2], red_sems.at[3], z_peer(k), MESH
         )
 
-    start_all(z_copy, nz, nz)
-    wait_later(zb.at[pl.ds(0, nz - 1)], red_sems.at[2], red_sems.at[3], "z")
+    @pl.when(owner)
+    def _():
+        wait_bytes(rs_recv.at[pl.ds(0, na - 1)], red_sems.at[1])
+        zb[zi] = jnp.sum(rs_recv[...].astype(F32), axis=0).astype(BF16)
+        start_all(z_copy, nz, nz)
+
+    pending.append(lambda: wait_if_owner(zb, red_sems.at[2], nz - 1, 0))
+
     for i in range(8):
         arrived(f"grad{i}")
     for r in range(D):
@@ -505,16 +555,18 @@
     cgr[row] = cgs[row]
     rgr[col] = rgs[col]
 
-    arrived("z")
-    ag[ai] = (jnp.sum(zb[...].astype(F32), axis=0) * (1.0 / bins)).astype(BF16)
-
     def ag_copy(k):
         return pltpu.make_async_remote_copy(
-            ag.at[ai], ag.at[ai], red_sems.at[4], red_sems.at[5], a_peer(k), MESH
-        )
-
-    start_all(ag_copy, na, nc)
-    wait_later(ag.at[pl.ds(0, na - 1)], red_sems.at[4], red_sems.at[5], "ag")
+            ag.at[chunk], ag.at[chunk], red_sems.at[4], red_sems.at[5], a_peer(k), MESH
+        )
+
+    @pl.when(owner)
+    def _():
+        wait_bytes(zb.at[pl.ds(0, nz - 1)], red_sems.at[3])
+        ag[chunk] = (jnp.sum(zb[...].astype(F32), axis=0) * (1.0 / bins)).astype(BF16)
+        start_all(ag_copy, na, nc)
+
+    pending.append(lambda: wait_if_owner(rs_recv, red_sems.at[4], na - 1, 0))
 
     for i in range(8):
         pg_ref[pl.ds(i * 8, 8)] = xs[pl.ds(i * 256, 256), :].reshape(8, TR, TC).astype(BF16)
@@ -524,17 +576,20 @@
     colg_ref[...] = jnp.sum(cgr[...], axis=0) * (1.0 / root)
     rowg_ref[...] = jnp.sum(rgr[...], axis=0)[:, :TR] * (1.0 / root)
 
-    arrived("ag")
-    total = ag[...].astype(F32)
-    low = total[:, :cr].reshape(256, TC)
-    high = total[:, cr:].reshape(256, TC)
+    wait_if_owner(ag, red_sems.at[5], owners - 1, owners)
+    total = ag[...].astype(F32).reshape(height * owners, TC)
     for p in range(3):
-        convg_ref[3 * p] = low[C * p : C * p + C, :C]
-        convg_ref[3 * p + 1] = low[C * p : C * p + C, C:]
-        convg_ref[3 * p + 2] = high[C * p : C * p + C, :C]
-    projg_ref[...] = high[3 * C :, C:]
-    gaing_ref[...] = jnp.sum(jnp.where(eye, high[:C, C : C + 1], 0.0), axis=0, keepdims=True)
-    shiftg_ref[...] = jnp.sum(jnp.where(eye, high[:C, C + 1 : C + 2], 0.0), axis=0, keepdims=True)
+        convg_ref[3 * p] = total[C * p : C * p + C, :C]
+        convg_ref[3 * p + 1] = total[C * p : C * p + C, C:]
+    high = total[3 * C : 3 * C + 96]
+    convg_ref[2] = high[:C, :C]
+    convg_ref[5, pl.ds(0, 32)] = high[C:, :C]
+    convg_ref[5, pl.ds(32, 32)] = high[:32, C:]
+    convg_ref[8] = high[32:, C:]
+    projg_ref[pl.ds(0, 32)] = total[288:320, :C]
+    projg_ref[pl.ds(32, 32)] = total[288:320, C:]
+    gaing_ref[...] = total[320:321, :C]
+    shiftg_ref[...] = total[320:321, C:]
 
     for wait in (*recvs.values(), *pending):
         wait()
@@ -552,7 +607,7 @@
 
 def shards(nr, nc, pair_in, row_feat, col_feat, cotangent, conv_weight, gain, shift, proj):
     na, nz = 4 * nc, nr // 4
-    cr = 256 // na
+    height, owners = chunking(na)
     hbm = pl.BlockSpec(memory_space=pltpu.HBM)
     vmem = pl.BlockSpec(memory_space=pltpu.VMEM)
     scratch = dict(
@@ -592,10 +647,10 @@
         kl=pltpu.VMEM((4, C, TC), BF16),
         kr=pltpu.VMEM((4, C, TC), BF16),
         wacc=pltpu.VMEM((4 * C, 4 * C), F32),
-        rs_send=pltpu.VMEM((na, 2 * cr, TC), BF16),
-        rs_recv=pltpu.VMEM((na, 2 * cr, TC), BF16),
-        zb=pltpu.VMEM((nz, 2 * cr, TC), BF16),
-        ag=pltpu.VMEM((na, 2 * cr, TC), BF16),
+        rs_send=pltpu.VMEM((owners, height, TC), BF16),
+        rs_recv=pltpu.VMEM((na, height, TC), BF16),
+        zb=pltpu.VMEM((nz, height, TC), BF16),
+        ag=pltpu.VMEM((owners, height, TC), BF16),
         cacc=pltpu.VMEM((C, TC), F32),
         cgs=pltpu.VMEM((nr, C // nr, TC), F32),
         cgr=pltpu.VMEM((nr, C // nr, TC), F32),

time: 43.5 us -> 43.2 us (level)
  no operation moved by 1% of the time
where the time goes in v5:
time: 43.2 us; the launch traced here: 43.1 us
  Pallas kernels  42.4 us (98%)
  between operations  0.64 us (1%)
    pallas_call x1, Pallas kernels, shards(): pl.pallas_call(functools.partial(kernel, nr, nc), out_shape=tuple((pltpu....  41.5 us
    pallas_call x1, Pallas kernels, shards(): pl.pallas_call(store_kernel, out_shape=shapes, in_specs=[vmem] * 7, out_s...  0.97 us

profile of v5, /device:TPU:1, one launch (start us, length us, event | category | flops | bytes accessed | tf_op | source)
XLA Modules:
  0.0 43.1 jit_solution(8402571077283529732)
XLA Ops:
  0.6 41.5 %shard_map.135 = (bf16[64,32,128]{2,1,0:T(8,128)(2,1)S(1)}, f32[8,32]{1,0:T(8,128)S(1)}, f32[2,128]{1,0:T(2,128)S(1)}, f32[9,64,64]{2,1,0:T(8,128)S(1)}, f32[64,...) custom-call(bf16[64,32,128]{2,1,0:T(8,128)(2,1)} %pair_in.1, bf16[8,32]{1,0:T(8,128)(2,1)} %rowf_in.1, ...), custom_call_target="tpu_custom_call" | custom-call | tf_op jit(solution)/shard_map/pallas_call | solution.py:678
  42.1 1.0 %shard_map.136 = (bf16[64,32,128]{2,1,0:T(8,128)(2,1)}, f32[8,32]{1,0:T(8,128)}, f32[2,128]{1,0:T(2,128)}, f32[9,64,64]{2,1,0:T(8,128)}, f32[64,64]{1,0:T(8,128)}, /*index=5*/f32[1,64]{1,0:T(1,128)}, f32[1,64]{1,0:T(1,128)}) custom-call(bf16[64,32,128]{2,1,0:T(8,128)(2,1)S(1)} %get-tuple-element.21.refs_0_, f32[8,32]{1,0:T(8,128)S(1)} %get-tuple-element.22.refs_1_, ...), custom_call_target="tpu_custom_call" | custom-call | tf_op jit(solution)/shard_map/pallas_call | solution.py:702
